TPU v7x, 128 devices: a whole 4x4x4 slice. The times are simulated.
128 devices in a mesh: ctx: 16 (over y, x_hi, core), fsdp: 8 (over z, x_lo).
Axes of the slice: x: 4 (x_hi: 2, x_lo: 2; x = x_hi * 2 + x_lo), y: 4, z: 4, core: 2. Of those that a mesh axis runs over, the one named last changes fastest.
Arguments:
- inputs: bfloat16 [8, 2048, 1024], P('fsdp', 'ctx'), may hold values from -4 to 4, as said below
- w_query: bfloat16 [1024, 1024], P('fsdp'), may hold values from -0.176776695 to 0.176776695
- b_query: bfloat16 [1024], P('fsdp'), may hold values from -4 to 4
- w_key: bfloat16 [1024, 1024], P('fsdp'), may hold values from -0.176776695 to 0.176776695
- w_value: bfloat16 [1024, 1024], P('fsdp'), may hold values from -0.1875 to 0.1875
- b_value: bfloat16 [1024], P('fsdp'), may hold values from -4 to 4
- w_out: bfloat16 [1024, 1024], P('fsdp'), may hold values from -6 to 6
- b_out: bfloat16 [1024], P('fsdp'), may hold values from -4 to 4
- gain_one: bfloat16 [1024], P('fsdp'), may hold values from 0.5 to 1.5
- shift_one: bfloat16 [1024], P('fsdp'), may hold values from -4 to 4
- w_up: bfloat16 [1024, 4096], P('fsdp'), may hold values from -0.1875 to 0.1875
- b_up: bfloat16 [4096], P('fsdp'), may hold values from -4 to 4
- w_down: bfloat16 [4096, 1024], P('fsdp'), may hold values from -0.125 to 0.125
- b_down: bfloat16 [1024], P('fsdp'), may hold values from -4 to 4
- gain_two: bfloat16 [1024], P('fsdp'), may hold values from 0.5 to 1.5
- shift_two: bfloat16 [1024], P('fsdp'), may hold values from -4 to 4
- cotangent: bfloat16 [8, 2048, 1024], P('fsdp', 'ctx'), may hold values from -6 to 6
Outputs:
- output: bfloat16 [8, 2048, 1024], P('fsdp', 'ctx')
- grad_inputs: float32 [8, 2048, 1024], P('fsdp', 'ctx')
- grad_w_query: float32 [1024, 1024], P('fsdp')
- grad_b_query: float32 [1024], P('fsdp')
- grad_w_key: float32 [1024, 1024], P('fsdp')
- grad_w_value: float32 [1024, 1024], P('fsdp')
- grad_b_value: float32 [1024], P('fsdp')
- grad_w_out: float32 [1024, 1024], P('fsdp')
- grad_b_out: float32 [1024], P('fsdp')
- grad_gain_one: float32 [1024], P('fsdp')
- grad_shift_one: float32 [1024], P('fsdp')
- grad_w_up: float32 [1024, 4096], P('fsdp')
- grad_b_up: float32 [4096], P('fsdp')
- grad_w_down: float32 [4096, 1024], P('fsdp')
- grad_b_down: float32 [1024], P('fsdp')
- grad_gain_two: float32 [1024], P('fsdp')
- grad_shift_two: float32 [1024], P('fsdp')
Inputs may be any that keep to these rules, and one draw needn't show every extreme that they name: `inputs`: independent entries of mean 0 and deviation 1.
All inputs are finite; a program needn't handle non-finite values.
Results may differ from a plain program's by a relative error of at most 0.024.
Values may be sent and summed in bfloat16 or wider, within the bound.
No kernel may reach another device: no remote copies, remote signals or barrier semaphores. Data moves between devices by JAX's collectives and lax.ppermute only.
A program may use at most 192 MiB of HBM per device.

v0:
```python
import functools

import jax
import jax.numpy as jnp
from jax import lax
from jax.experimental import pallas as pl
from jax.experimental.pallas import tpu as pltpu
from jax.sharding import PartitionSpec as P

EPSILON = 1e-05
LOW = jnp.bfloat16
F32 = jnp.float32
WIDTH = 1024
HEAD = 64
ROWS = 128
LENGTH = 2048
CHUNK = 512
QUERIES = 256
SAME_CORE = [list(range(0, 16, 2)), list(range(1, 16, 2))]
SAME_QUARTER = [
    [(high * 2 + low) * 4 + x * 2 + core for high in range(2) for x in range(2)]
    for low in range(2)
    for core in range(2)
]
CORE, FAR_X, NEAR_Y = 1, 2, 4
VMEM_LIMIT = 50 * 1024 * 1024


def swap(block, bit):
    return lax.ppermute(block, "ctx", [(i, i ^ bit) for i in range(16)])


def along_y(block, steps):
    return lax.ppermute(block, "ctx", [(i, (i + 4 * steps) % 16) for i in range(16)])


def along_z(block, steps):
    return lax.ppermute(block, "fsdp", [(i, (i + 2 * steps) % 8) for i in range(8)])


def along_x(block):
    return lax.ppermute(block, "fsdp", [(i, i ^ 1) for i in range(8)])


def exchange(blocks, axis, groups=None):
    return lax.all_to_all(blocks, axis, 0, 0, axis_index_groups=groups, tiled=True)


def after(block, other):
    return lax.optimization_barrier((block, other))[0]


def repeated(block, count):
    return jnp.broadcast_to(block[None], (count,) + block.shape)


def dims(matrix, other, left, right):
    return lax.dot_general(
        matrix, other, (((left,), (right,)), ((), ())), preferred_element_type=F32
    )


def dot(matrix, other):
    return dims(matrix, other, 1, 0)


def split_low(value):
    high = value.astype(LOW)
    return high, (value - high.astype(F32)).astype(LOW)


def norm_forward(hidden, gain, shift):
    center = hidden - jnp.mean(hidden, axis=-1, keepdims=True)
    scale = lax.rsqrt(jnp.mean(center * center, axis=-1, keepdims=True) + EPSILON)
    unit = center * scale
    return unit * gain + shift, unit, scale


def norm_backward(grad, unit, scale, gain):
    inner = grad * gain
    mean_inner = jnp.mean(inner, axis=-1, keepdims=True)
    mean_unit = jnp.mean(inner * unit, axis=-1, keepdims=True)
    back = scale * (inner - mean_inner - unit * mean_unit)
    return back, jnp.sum(grad * unit, axis=0), jnp.sum(grad, axis=0)


def pack_kernel(ctx, w_query, w_key, w_value, vectors, heads, turned):
    at = ctx[0]
    for index, ref in enumerate((w_query, w_key, w_value)):
        pair = ref[:, pl.ds(pl.multiple_of((at >> 1) * ROWS, ROWS), ROWS)]
        turned[...] = pair.astype(F32).T
        column = turned[pl.ds(pl.multiple_of((at & 1) * HEAD, HEAD), HEAD), :].astype(LOW)
        for f in range(8):
            heads[f, index * HEAD : (index + 1) * HEAD, :] = column
    for f in range(8):
        heads[f, 3 * HEAD :, :] = vectors[...]


def weights_kernel(ctx, w_out, w_up, w_down, early, late):
    at = ctx[0]
    core = at & 1
    quarter = ((at >> 2) & 1) * 2 + core
    for f in range(8):
        early[f, :64, :] = w_out[pl.ds(pl.multiple_of(core * 64, 64), 64), :]
        late[f] = w_down[pl.ds(pl.multiple_of(quarter * ROWS, ROWS), ROWS), :]
        for block in range(8):
            span = pl.ds(pl.multiple_of(block * 512 + quarter * ROWS, ROWS), ROWS)
            early[f, 64:, block * ROWS : (block + 1) * ROWS] = w_up[:, span]


def forward_kernel(order, *refs):
    parts = refs[:8]
    w_ref, bias_q, bias_v, qkv, rows, mixed_low, mixed, total, own_weight, held = refs[8:]
    weight = jnp.concatenate([w_ref[f, : 3 * HEAD, :] for f in range(8)], axis=1)
    own_weight[...] = weight
    for index in range(LENGTH // QUERIES):
        span = slice(index * QUERIES, (index + 1) * QUERIES)
        product = dims(weight, parts[index][...], 1, 1)
        query = (product[:HEAD] + bias_q[...]) * (HEAD**-0.5)
        value = product[2 * HEAD :] + bias_v[...]
        pair = jnp.concatenate([product[HEAD : 2 * HEAD], value], axis=0)
        qkv[:HEAD, span] = query.astype(LOW)
        qkv[HEAD:, span] = pair.astype(LOW)
        rows[span, :] = pair.T.astype(LOW)

    def step(index, carry):
        span = pl.ds(pl.multiple_of(index * QUERIES, QUERIES), QUERIES)
        query = qkv[:HEAD, span]
        padded = jnp.concatenate([query, jnp.zeros_like(query)], axis=0)
        peak = None
        for at in range(0, LENGTH, CHUNK):
            scores = dot(rows[at : at + CHUNK, :], padded)
            held[at : at + CHUNK, :] = scores
            top = jnp.max(scores, axis=0, keepdims=True)
            peak = top if peak is None else jnp.maximum(peak, top)
        weight_sum = jnp.zeros((1, QUERIES), F32)
        acc = jnp.zeros((HEAD, QUERIES), F32)
        for at in range(0, LENGTH, CHUNK):
            weights = jnp.exp(held[at : at + CHUNK, :] - peak)
            weight_sum += jnp.sum(weights, axis=0, keepdims=True)
            acc += dot(qkv[2 * HEAD :, at : at + CHUNK], weights.astype(LOW))
        acc = acc / weight_sum
        mixed[:, span] = acc
        total[:, span] = peak + jnp.log(weight_sum)
        mixed_low[order[2 * index]] = acc[:, :ROWS].astype(LOW)
        mixed_low[order[2 * index + 1]] = acc[:, ROWS:].astype(LOW)
        return carry

    lax.fori_loop(0, LENGTH // QUERIES, step, 0)


def backward_kernel(order, grad_ref, qkv, rows, mixed, total, *refs):
    parts, weight = refs[:8], refs[8]
    message, shares = refs[9], refs[10:18]
    kept, key_acc, value_acc = refs[18:]
    key_acc[...] = jnp.zeros_like(key_acc)
    value_acc[...] = jnp.zeros_like(value_acc)

    def step(index, carry):
        span = pl.ds(pl.multiple_of(index * QUERIES, QUERIES), QUERIES)
        first, second = order[2 * index], order[2 * index + 1]
        query = qkv[:HEAD, span]
        grad = jnp.concatenate([grad_ref[first], grad_ref[second]], axis=1)
        delta = jnp.sum(grad.astype(F32) * mixed[:, span], axis=0, keepdims=True)
        log_total = total[:, span]
        query_pad = jnp.concatenate([query, jnp.zeros_like(query)], axis=0)
        grad_pad = jnp.concatenate([jnp.zeros_like(grad), grad], axis=0)
        query_grad = jnp.zeros((HEAD, QUERIES), F32)
        for at in range(0, LENGTH, CHUNK):
            block = rows[at : at + CHUNK, :]
            chances = jnp.exp(dot(block, query_pad) - log_total)
            chance_grad = dot(block, grad_pad)
            score_grad = (chances * (chance_grad - delta)).astype(LOW)
            value_acc[:, at : at + CHUNK] += dims(grad, chances.astype(LOW), 1, 1)
            key_acc[:, at : at + CHUNK] += dims(query, score_grad, 1, 1)
            query_grad += dot(qkv[HEAD : 2 * HEAD, at : at + CHUNK], score_grad)
        kept[:HEAD, span] = (query_grad * (HEAD**-0.5)).astype(LOW)
        return carry

    lax.fori_loop(0, LENGTH // QUERIES, step, 0)
    kept[HEAD : 2 * HEAD, :] = key_acc[...].astype(LOW)
    kept[2 * HEAD :, :] = value_acc[...].astype(LOW)
    acc = None
    for index in range(LENGTH // QUERIES):
        span = slice(index * QUERIES, (index + 1) * QUERIES)
        term = dot(kept[:, span], parts[index][...])
        acc = term if acc is None else acc + term
    sums = dims(jnp.ones((8, LENGTH), LOW), kept[...], 1, 1)[:1]
    sums = jnp.concatenate([sums, jnp.zeros((1, HEAD), F32)], axis=1)
    high = sums.astype(LOW).astype(F32)
    tail = jnp.concatenate([high, sums - high, jnp.zeros((1, 512), F32)], axis=1)
    tail = jnp.concatenate([tail, jnp.zeros((7, WIDTH), F32)], axis=0)
    for f in range(8):
        span = slice(f * ROWS, (f + 1) * ROWS)
        wide = jnp.concatenate([acc[j * 24 : (j + 1) * 24, span] for j in range(8)], axis=1)
        message[f] = jnp.concatenate([wide, tail], axis=0).astype(LOW)
    for index, share in enumerate(shares):
        span = slice(index * QUERIES, (index + 1) * QUERIES)
        share[...] = dims(kept[:, span], weight[...], 0, 0).astype(LOW)


def quarter_kernel(out, sums_ref, message):
    for e in range(4):
        rows = [out[f, e * 16 : (e + 1) * 16, :] for f in range(8)]
        message[e, :128, :] = jnp.concatenate(rows, axis=0).astype(LOW)
        sums = sums_ref[e]
        high = sums.astype(LOW).astype(F32)
        tail = jnp.concatenate([high, sums - high], axis=0)
        message[e, 128:, :] = tail.astype(LOW)


def extra_kernel(ctx, found, heads, message):
    piece = (ctx[0] >> 3) * 2 + ((ctx[0] >> 1) & 1)
    total = found[0].astype(F32)
    for index in range(1, 4):
        total += found[index].astype(F32)
    sums = total[128:136] + total[136:144]
    for f in range(8):
        row = jnp.where(f >> 1 == piece, sums[f & 1 : (f & 1) + 1], 0.0)
        high = row.astype(LOW).astype(F32)
        tail = jnp.concatenate([high, row - high, jnp.zeros((14, WIDTH), F32)], axis=0)
        message[f, :32, :] = heads[f]
        message[f, 32:48, :] = total[f * 16 : (f + 1) * 16].astype(LOW)
        message[f, 48:, :] = tail.astype(LOW)


def assembly_kernel(ctx, mine, theirs, down, up, out, query, key, value):
    core = ctx[0] & 1
    for side, ref in enumerate((mine, theirs)):
        place = core if side == 0 else 1 - core
        for e in range(8):
            high, low, x = e >> 2, (e >> 1) & 1, e & 1
            part, quarter = high * 2 + x, low * 2 + place
            row = pl.multiple_of(quarter * ROWS + part * 32, 32)
            down[pl.ds(row, 32), :] = ref[e, :32, :].astype(F32)
            block = ref[e, 32:64, :].astype(F32)
            for f in range(8):
                span = pl.ds(pl.multiple_of(f * 512 + quarter * ROWS, ROWS), ROWS)
                up[part * 32 : (part + 1) * 32, span] = block[:, f * ROWS : (f + 1) * ROWS]
            if low == 0:
                row = pl.multiple_of(place * 64 + part * 16, 16)
                pair = ref[e, 64:80, :].astype(F32) + ref[e + 2, 64:80, :].astype(F32)
                out[pl.ds(row, 16), :] = pair
    for e in range(8):
        own = mine[e, 80:112, :].astype(F32)[:24]
        other = theirs[e, 80:112, :].astype(F32)[:24]
        pair = []
        for wide in (jnp.where(core == 0, own, other), jnp.where(core == 0, other, own)):
            pair.append(
                jnp.concatenate([wide[:, j * ROWS : (j + 1) * ROWS] for j in range(8)], axis=0)
            )
        for index, ref in enumerate((query, key, value)):
            rows = slice(index * HEAD, (index + 1) * HEAD)
            both = jnp.concatenate([pair[0][rows], pair[1][rows]], axis=0)
            ref[:, e * ROWS : (e + 1) * ROWS] = both.T


def call(kernel, outs, scratch, flops, moved, *operands):
    in_specs = [pl.BlockSpec(memory_space=pltpu.SMEM if operand.dtype == jnp.int32 else pltpu.VMEM) for operand in operands]
    return pl.pallas_call(
        kernel,
        out_shape=[jax.ShapeDtypeStruct(shape, dtype) for shape, dtype in outs],
        in_specs=in_specs,
        out_specs=[pl.BlockSpec(memory_space=pltpu.VMEM)] * len(outs),
        scratch_shapes=scratch,
        compiler_params=pltpu.CompilerParams(vmem_limit_bytes=VMEM_LIMIT),
        cost_estimate=pl.CostEstimate(flops=flops, bytes_accessed=moved, transcendentals=0),
    )(*operands)


def on_device(
    inputs,
    w_query,
    b_query,
    w_key,
    w_value,
    b_value,
    w_out,
    b_out,
    gain_one,
    shift_one,
    w_up,
    b_up,
    w_down,
    b_down,
    gain_two,
    shift_two,
    cotangent,
):
    ctx, fsdp = lax.axis_index("ctx"), lax.axis_index("fsdp")
    core = ctx & 1

    vectors = jnp.concatenate(
        [
            jnp.stack([b_query, b_value, b_out, gain_one, shift_one, b_down, gain_two, shift_two]),
            b_up.reshape(4, ROWS),
            jnp.zeros((4, ROWS), LOW),
        ]
    )
    at = ctx.reshape(1).astype(jnp.int32)
    (heads,) = call(
        pack_kernel,
        [((8, 208, ROWS), LOW)],
        [pltpu.VMEM((ROWS, ROWS), F32)],
        10**6,
        10**6,
        at,
        w_query,
        w_key,
        w_value,
        vectors,
    )
    own = after(inputs.reshape(ROWS, WIDTH), heads)
    heads = exchange(heads, "fsdp")
    pair = jnp.concatenate([own, swap(own, FAR_X)], axis=0)
    pair = after(pair, heads)
    parts = [pair] + [along_y(pair, k) for k in (1, 2, 3)]
    parts = parts + [swap(part, CORE) for part in parts]
    order = jnp.stack(
        [
            (((ctx >> 2) - k) % 4) * 4 + ((ctx & 3) ^ (2 * j + s))
            for s in range(2)
            for k in range(4)
            for j in range(2)
        ]
    ).astype(jnp.int32)

    early, late = call(
        weights_kernel,
        [((8, 64 + ROWS, WIDTH), LOW), ((8, ROWS, WIDTH), LOW)],
        [],
        10**6,
        10**7,
        at,
        w_out,
        w_up,
        w_down,
    )
    early = exchange(after(early, pair), "fsdp")
    vecs = heads[:, 3 * HEAD :, :].astype(F32)

    def whole(index):
        return vecs[:, index, :].reshape(WIDTH)

    vec_query, vec_value, vec_out, gain_a, shift_a, vec_down, gain_b, shift_b = (
        whole(index) for index in range(8)
    )
    quarter = ((ctx >> 2) & 1) * 2 + core
    vec_up = lax.dynamic_slice(vecs, (0, 8 + quarter, 0), (8, 1, ROWS)).reshape(WIDTH)
    bias_q = lax.dynamic_slice(vec_query, (ctx * HEAD,), (HEAD,)).reshape(HEAD, 1)
    bias_v = lax.dynamic_slice(vec_value, (ctx * HEAD,), (HEAD,)).reshape(HEAD, 1)

    def pick(block, index, axis):
        return lax.dynamic_index_in_dim(block, index, axis, keepdims=False)

    def by_core(mine, theirs, axis):
        first, second = jnp.where(core == 0, mine, theirs), jnp.where(core == 0, theirs, mine)
        return jnp.stack([first, second], axis=axis)

    qkv, rows, mixed_low, mixed, total, own_weight = call(
        forward_kernel,
        [
            ((3 * HEAD, LENGTH), LOW),
            ((LENGTH, 2 * HEAD), LOW),
            ((16, HEAD, ROWS), LOW),
            ((HEAD, LENGTH), F32),
            ((1, LENGTH), F32),
            ((3 * HEAD, WIDTH), LOW),
        ],
        [pltpu.VMEM((LENGTH, QUERIES), F32)],
        10**10,
        10**7,
        order,
        *parts,
        heads,
        bias_q,
        bias_v,
    )
    early, mixed_low = lax.optimization_barrier((early, mixed_low))
    context = exchange(mixed_low, "ctx")
    out_mine = early[:, :64].reshape(512, WIDTH)
    out_theirs = swap(out_mine, CORE)
    mat_up = early[:, 64:].reshape(WIDTH, WIDTH)
    mat_down = exchange(after(late, context), "fsdp").reshape(WIDTH, WIDTH)
    context_mine = pick(context.reshape(8, 2, HEAD, ROWS), core, 1).reshape(512, ROWS)
    context_theirs = pick(context.reshape(8, 2, HEAD, ROWS), 1 - core, 1).reshape(512, ROWS)
    context = context.reshape(WIDTH, ROWS)

    def share(block):
        block = jnp.concatenate([block, swap(block, NEAR_Y)], axis=0)
        return jnp.concatenate([block, swap(block, CORE)], axis=0)

    def collect(partial):
        half = partial[: 2 * ROWS] + swap(partial[2 * ROWS :].astype(LOW), CORE).astype(F32)
        return half[:ROWS] + swap(half[ROWS:].astype(LOW), NEAR_Y).astype(F32)

    branch = dims(context_mine, out_mine, 0, 0) + dims(context_theirs, out_theirs, 0, 0) + vec_out
    first, unit_one, scale_one = norm_forward(own.astype(F32) + branch, gain_a, shift_a)
    first_all = share(first.astype(LOW))
    hidden = dot(first_all, mat_up) + vec_up
    gate = 0.5 * (1.0 + lax.erf(hidden * (0.5**0.5)))
    slope = gate + hidden * jnp.exp(-0.5 * hidden * hidden) * 0.3989422804014327
    active = (hidden * gate).astype(LOW)
    second = collect(dot(active, mat_down)) + vec_down
    result, unit_two, scale_two = norm_forward(first + second, gain_b, shift_b)

    grad_out = cotangent.reshape(ROWS, WIDTH).astype(F32)
    grad_two, grad_gain_b, grad_shift_b = norm_backward(grad_out, unit_two, scale_two, gain_b)
    grad_second = grad_two.astype(LOW)
    grad_vec_down = jnp.sum(grad_second.astype(F32), axis=0)
    second_all = share(grad_second)
    down = dims(active, second_all, 0, 0).astype(LOW).reshape(4, 2, ROWS, WIDTH)
    z, low_x, low_y = fsdp >> 1, fsdp & 1, (ctx >> 2) & 1
    down_found = [along_z(pick(down, (z + k) % 4, 0), k) for k in (1, 3, 2)]
    grad_hidden = (slope * dims(second_all, mat_down, 1, 1)).astype(LOW)
    grad_vec_up = jnp.sum(grad_hidden.astype(F32), axis=0)
    up = dims(first_all, grad_hidden, 0, 0).astype(LOW).reshape(4, 2, ROWS, WIDTH)
    grad_first = grad_two + collect(dims(grad_hidden, mat_up, 1, 1))
    grad_first = after(grad_first, (up, down_found[:2]))
    grad_one, grad_gain_a, grad_shift_a = norm_backward(grad_first, unit_one, scale_one, gain_a)
    grad_branch = grad_one.astype(LOW)
    grad_vec_out = jnp.sum(grad_branch.astype(F32), axis=0)
    grad_context = by_core(
        dims(out_mine, grad_branch, 1, 1).reshape(8, HEAD, ROWS),
        dims(out_theirs, grad_branch, 1, 1).reshape(8, HEAD, ROWS),
        1,
    )
    grad_context = grad_context.astype(LOW).reshape(16, HEAD, ROWS)
    grad_heads = exchange(grad_context, "ctx")
    out = dot(after(context, grad_context), grad_branch).astype(LOW).reshape(8, 2, 64, WIDTH)
    out = pick(out, core, 1).astype(F32) + swap(pick(out, 1 - core, 1), CORE).astype(F32)
    sums = jnp.stack(
        [
            grad_vec_out,
            grad_gain_a,
            grad_shift_a,
            grad_vec_down,
            grad_gain_b,
            grad_shift_b,
            grad_vec_up,
            jnp.zeros_like(grad_vec_up),
        ]
    )
    sums = sums.reshape(8, 4, 2, ROWS).transpose(1, 2, 0, 3).reshape(4, 2, WIDTH)
    sums = jnp.concatenate([sums, jnp.zeros((4, 6, WIDTH), F32)], axis=1)
    (quarter_message,) = call(
        quarter_kernel, [((4, 144, WIDTH), LOW)], [], 10**6, 10**6, out, sums
    )
    summed = exchange(after(quarter_message, grad_heads), "ctx", SAME_QUARTER)
    grad_heads = after(grad_heads, quarter_message)
    message, *shares = call(
        backward_kernel,
        [((8, 32, WIDTH), LOW)] + [((QUERIES, WIDTH), LOW)] * 8,
        [pltpu.VMEM((3 * HEAD, LENGTH), LOW), pltpu.VMEM((HEAD, LENGTH), F32), pltpu.VMEM((HEAD, LENGTH), F32)],
        10**6,
        10**5,
        order,
        grad_heads,
        qkv,
        rows,
        mixed,
        total,
        *parts,
        own_weight,
    )
    up_found = [along_z(pick(up, (z + k) % 4, 0), k) for k in (1, 3, 2)]
    down_found = after([*down_found[:2], after(down_found[2], grad_context)], message)
    theirs = [swap(share, CORE) for share in shares[4:]]
    message = after(message, up_found)
    (message,) = call(
        extra_kernel, [((8, 64, WIDTH), LOW)], [], 10**6, 10**6, at, summed, message
    )
    shares, theirs = after((shares, theirs), message)
    def own_sum(blocks, found):
        total = pick(blocks, z, 0).astype(F32)
        for part in found:
            total += part.astype(F32)
        return pick(total, low_x, 0), along_x(pick(total, 1 - low_x, 0).astype(LOW))

    down, down_found = own_sum(down, down_found)
    down += after(down_found, message).astype(F32)
    up, up_found = own_sum(up, after(up_found, message))
    up += up_found.astype(F32)

    summed = jnp.sum(exchange(message, "fsdp").astype(F32), axis=0)

    shares = [mine.astype(F32) + other.astype(F32) for mine, other in zip(shares[:4], theirs)]
    pair, sent = shares[0], [share.astype(LOW) for share in shares[1:]]
    found = [along_y(sent[k - 1], -k) for k in (1, 3, 2)]

    hidden_rows = jnp.concatenate(
        [down.reshape(4, 32, WIDTH).astype(LOW), up.reshape(4, 32, WIDTH).astype(LOW)], axis=1
    )
    hidden_rows = after(hidden_rows, summed)
    found = after(found, hidden_rows)
    for part in found:
        pair += part.astype(F32)
    grad_in = grad_one + pair[:ROWS] + swap(pair[ROWS:].astype(LOW), FAR_X).astype(F32)
    hidden_rows = exchange(hidden_rows, "ctx", SAME_QUARTER)
    hidden_rows = jnp.sum(hidden_rows.astype(F32), axis=0)
    head_sums = summed[24:25, :512]
    head_sums = head_sums[:, :256] + head_sums[:, 256:]
    head_sums = jnp.concatenate([head_sums, jnp.zeros((1, 768), F32)], axis=1)

    message = jnp.concatenate(
        [
            hidden_rows.astype(LOW),
            summed[32:48].astype(LOW),
            summed[:24].astype(LOW),
            *split_low(head_sums),
            *split_low(summed[48:49] + summed[49:50]),
            jnp.zeros((4, WIDTH), LOW),
        ],
        axis=0,
    )
    message = after(message, pair)
    shared = exchange(repeated(message, 8), "ctx", SAME_CORE)
    shared = after(shared, grad_in)
    shared_theirs = swap(shared, CORE)
    square = ((ROWS, WIDTH), F32)
    grad_mat_down, grad_mat_up, grad_mat_out, grad_mat_query, grad_mat_key, grad_mat_value = call(
        assembly_kernel,
        [((512, WIDTH), F32), ((ROWS, 4096), F32), square, square, square, square],
        [],
        10**6,
        10**7,
        at,
        shared,
        shared_theirs,
    )

    def joined(block):
        return block[0].astype(F32) + block[1].astype(F32)

    holder = (z >> 1) * 4 + (z & 1)
    sums = jnp.stack([joined(pick(shared, holder + e, 0)[106:108]) for e in (0, 2)])
    sums_theirs = jnp.stack([joined(pick(shared_theirs, holder + e, 0)[106:108]) for e in (0, 2)])
    sums = by_core(sums, sums_theirs, 1).reshape(4, 8, ROWS)
    grad_vec_up = sums[:, 6].reshape(512)
    vector_grads = jnp.sum(sums[:, :6], axis=0)
    head_sums = by_core(pick(shared, fsdp, 0)[104:106], pick(shared_theirs, fsdp, 0)[104:106], 0)
    head_sums = (head_sums[:, 0].astype(F32) + head_sums[:, 1].astype(F32)).reshape(2, 8, ROWS)
    grad_vec_query = head_sums[:, 0, :HEAD].reshape(ROWS)
    grad_vec_value = head_sums[:, 1, :HEAD].reshape(ROWS)

    return (
        result.reshape(1, ROWS, WIDTH).astype(LOW),
        grad_in.reshape(1, ROWS, WIDTH),
        grad_mat_query,
        grad_vec_query,
        grad_mat_key,
        grad_mat_value,
        grad_vec_value,
        grad_mat_out,
        vector_grads[0],
        vector_grads[1],
        vector_grads[2],
        grad_mat_up,
        grad_vec_up,
        grad_mat_down,
        vector_grads[3],
        vector_grads[4],
        vector_grads[5],
    )


def solution(mesh):
    tokens, matrix, vector = P("fsdp", "ctx", None), P("fsdp", None), P("fsdp")
    return jax.shard_map(
        on_device,
        mesh=mesh,
        in_specs=(
            tokens,
            matrix,
            vector,
            matrix,
            matrix,
            vector,
            matrix,
            vector,
            vector,
            vector,
            matrix,
            vector,
            matrix,
            vector,
            vector,
            vector,
            tokens,
        ),
        out_specs=(
            tokens,
            tokens,
            matrix,
            vector,
            matrix,
            matrix,
            vector,
            matrix,
            vector,
            vector,
            vector,
            matrix,
            vector,
            matrix,
            vector,
            vector,
            vector,
        ),
        check_vma=False,
    )
```

profile of v0, /device:TPU:1, one launch (start us, length us, event | category | flops | bytes accessed | tf_op | source)
XLA Modules:
  0.0 322.0 jit_solution(9645050443334388452)
XLA Ops:
  0.7 1.6 concatenate.61.vectors
  6.1 3.6 %collective-permute-start = (bf16[128,1024]{1,0:T(8,128)(2,1)}, bf16[128,1024]{1,0:T(8,128)(2,1)S(1)}, u32[]{:S(2)}, u32[]{:S(2)}) collective-permute-start(bf16[128,1024]{1,0:T(8,128)(2,1)} %bitcast.186), channel_id=1, source_target_pairs={{0,16},{8,24},{16,0},{24,8},{32,48},{40,56},{48,32},{56,40},{64,80... | collective-permute-start | bytes 786440 | tf_op jit(solution)/shard_map/ppermute | solution.py:30
  9.7 5.1 %all-to-all-start = ((bf16[8,208,128]{2,1,0:T(8,128)(2,1)}), bf16[8,208,128]{2,1,0:T(8,128)(2,1)S(1)}, u32[]{:S(2)}, u32[]{:S(2)}) async-start(bf16[8,208,128]{2,1,0:T(8,128)(2,1)} %shard_map.296), calls=%async_computation | async-start | bytes 851968 | tf_op jit(solution)/shard_map/all_to_all | solution.py:46
  15.7 3.0 shard_map.297
  18.8 5.0 %all-to-all-done.refs_8_ = bf16[8,208,128]{2,1,0:T(8,128)(2,1)S(1)} async-done(((bf16[8,208,128]{2,1,0:T(8,128)(2,1)}), bf16[8,208,128]{2,1,0:T(8,128)(2,1)S(1)}, u32[]{:S(2)}, u32[]{:S(2)}) %all-to-all-start) | async-done | bytes 426016 | tf_op jit(solution)/shard_map/all_to_all | solution.py:46
  23.8 4.5 %all-to-all-start.1 = ((bf16[8,192,1024]{2,1,0:T(8,128)(2,1)}), bf16[8,192,1024]{2,1,0:T(8,128)(2,1)}, u32[]{:S(2)}, u32[]{:S(2)}) async-start(bf16[8,192,1024]{2,1,0:T(8,128)(2,1)} %get-tuple-element.76), calls=%async_computation.1 | async-start | bytes 6291456 | tf_op jit(solution)/shard_map/all_to_all | solution.py:46
  28.3 1.4 collective-permute-start.1
  29.6 2.6 collective-permute-start.2
  33.4 2.6 collective-permute-start.4
  36.0 5.5 %collective-permute-done.1.refs_1_ = bf16[256,1024]{1,0:T(8,128)(2,1)S(1)} collective-permute-done((bf16[256,1024]{1,0:T(8,128)(2,1)S(1)}, bf16[256,1024]{1,0:T(8,128)(2,1)S(1)}, u32[]{:S(2)}, u32[]{:S(2)}) %collective-permute-start.1) | collective-permute-done | bytes 524320 | tf_op jit(solution)/shard_map/ppermute | solution.py:34
  41.5 3.5 %collective-permute-start.5 = (bf16[256,1024]{1,0:T(8,128)(2,1)S(1)}, bf16[256,1024]{1,0:T(8,128)(2,1)}, u32[]{:S(2)}, u32[]{:S(2)}) collective-permute-start(bf16[256,1024]{1,0:T(8,128)(2,1)S(1)} %collective-permute-done.1.refs_1_), channel_id=1, source_target_pairs={{0,8},{8,0},{16,24},{24,16},{32,40},{40,32},{48,56},{56,48},{64,72... | collective-permute-start | bytes 1572872 | tf_op jit(solution)/shard_map/ppermute | solution.py:30
  45.0 8.9 %collective-permute-done.2.refs_2_ = bf16[256,1024]{1,0:T(8,128)(2,1)S(1)} collective-permute-done((bf16[256,1024]{1,0:T(8,128)(2,1)S(1)}, bf16[256,1024]{1,0:T(8,128)(2,1)S(1)}, u32[]{:S(2)}, u32[]{:S(2)}) %collective-permute-start.2) | collective-permute-done | bytes 524320 | tf_op jit(solution)/shard_map/ppermute | solution.py:34
  53.9 2.5 collective-permute-start.6
  58.8 13.9 %shard_map.298 = (bf16[192,2048]{1,0:T(8,128)(2,1)}, bf16[2048,128]{1,0:T(8,128)(2,1)S(1)}, bf16[16,64,128]{2,1,0:T(8,128)(2,1)}, f32[64,2048]{1,0:T(8,128)S(1)}...) custom-call(s32[16]{0:T(128)S(1)} %stack.155.order, bf16[256,1024]{1,0:T(8,128)(2,1)S(1)} %pad_maximum_fusion.2.refs_0_, ...), custom_call_target="tpu_custom_call" | custom-call | flops 10000000000 | bytes 10000000 | tf_op jit(solution)/shard_map/pallas_call | solution.py:260
  74.3 1.4 slice.186
  76.2 4.7 %all-to-all-start.2 = ((bf16[16,64,128]{2,1,0:T(8,128)(2,1)}), bf16[16,64,128]{2,1,0:T(8,128)(2,1)S(1)}, u32[]{:S(2)}, u32[]{:S(2)}) async-start(bf16[16,64,128]{2,1,0:T(8,128)(2,1)} %get-tuple-element.78), calls=%async_computation.2 | async-start | bytes 524288 | tf_op jit(solution)/shard_map/all_to_all | solution.py:46
  80.9 8.7 %all-to-all-done.2 = bf16[16,64,128]{2,1,0:T(8,128)(2,1)S(1)} async-done(((bf16[16,64,128]{2,1,0:T(8,128)(2,1)}), bf16[16,64,128]{2,1,0:T(8,128)(2,1)S(1)}, u32[]{:S(2)}, u32[]{:S(2)}) %all-to-all-start.2) | async-done | bytes 262176 | tf_op jit(solution)/shard_map/all_to_all | solution.py:46
  89.6 4.4 %all-to-all-start.3 = ((bf16[8,128,1024]{2,1,0:T(8,128)(2,1)}), bf16[8,128,1024]{2,1,0:T(8,128)(2,1)}, u32[]{:S(2)}, u32[]{:S(2)}) async-start(bf16[8,128,1024]{2,1,0:T(8,128)(2,1)} %get-tuple-element.81), calls=%async_computation.3 | async-start | bytes 4194304 | tf_op jit(solution)/shard_map/all_to_all | solution.py:46
  96.1 6.4 %collective-permute-done.9 = bf16[128,1024]{1,0:T(8,128)(2,1)S(1)} collective-permute-done((bf16[128,1024]{1,0:T(8,128)(2,1)S(1)}, bf16[128,1024]{1,0:T(8,128)(2,1)S(1)}, u32[]{:S(2)}, u32[]{:S(2)}) %collective-permute-start.9) | collective-permute-done | bytes 262176 | tf_op jit(solution)/shard_map/ppermute | solution.py:30
  102.5 2.2 collective-permute-start.10
  104.7 1.8 slice.190
  107.8 3.6 %multiply_convert_fusion = (bf16[512,1024]{1,0:T(8,128)(2,1)}, f32[512,1024]{1,0:T(8,128)}) fusion(f32[1024]{0:T(1024)S(1)} %bitcast.216, bf16[1024,1024]{1,0:T(8,128)(2,1)S(1)} %bitcast.182, bf16[256,1024]{1,0:T(8,128)(2,1)S(1)} %collective-permute-done.10, bf16[128,1024]{1,0:T(8,128)(2,1)S(1)} %collective-permute-done.9, bf16[128,1024]{1,0:T(8,128)(2,1)S(1)} %fusion.27), kind=kOutput, calls=%fused_computation.10 | convolution fusion | flops 1080033280 | bytes 6295552 | tf_op jit(solution)/shard_map/dot_general | solution.py:58
  111.4 8.4 %all-to-all-done.3 = bf16[8,128,1024]{2,1,0:T(8,128)(2,1)} async-done(((bf16[8,128,1024]{2,1,0:T(8,128)(2,1)}), bf16[8,128,1024]{2,1,0:T(8,128)(2,1)}, u32[]{:S(2)}, u32[]{:S(2)}) %all-to-all-start.3) | async-done | bytes 2097184 | tf_op jit(solution)/shard_map/all_to_all | solution.py:46
  119.8 3.2 fusion.64
  123.1 2.3 collective-permute-start.11
  125.4 1.5 collective-permute-done.11
  127.6 7.2 %collective-permute-done.12 = bf16[128,1024]{1,0:T(8,128)(2,1)S(1)} collective-permute-done((bf16[128,1024]{1,0:T(8,128)(2,1)S(1)}, bf16[128,1024]{1,0:T(8,128)(2,1)S(1)}, u32[]{:S(2)}, u32[]{:S(2)}) %collective-permute-start.12) | collective-permute-done | bytes 262176 | tf_op jit(solution)/shard_map/ppermute | solution.py:30
  136.3 6.3 %collective-permute-done.13 = bf16[128,1024]{1,0:T(8,128)(2,1)S(1)} collective-permute-done((bf16[128,1024]{1,0:T(8,128)(2,1)S(1)}, bf16[128,1024]{1,0:T(8,128)(2,1)S(1)}, u32[]{:S(2)}, u32[]{:S(2)}) %collective-permute-start.13) | collective-permute-done | bytes 262176 | tf_op jit(solution)/shard_map/ppermute | solution.py:30
  142.6 2.2 collective-permute-start.14
  144.8 1.5 collective-permute-done.14
  146.4 4.8 %convert_reduce_fusion.1 = (f32[1024]{0:T(1024)S(1)}, bf16[512,1024]{1,0:T(8,128)(2,1)S(1)}) fusion(bf16[1024,1024]{1,0:T(8,128)(2,1)} %bitcast.40, bf16[256,1024]{1,0:T(8,128)(2,1)S(1)} %collective-permute-done.14, bf16[128,1024]{1,0:T(8,128)(2,1)S(1)} %collective-permute-done.13, bf16[128,1024]{1,0:T(8,128)(2,1)S(1)} %get-tuple-element.137, ...), kind=kOutput, calls=%fused_computation.9 | convolution fusion | flops 1083702272 | bytes 6299648 | tf_op jit(solution)/shard_map/dot_general | solution.py:58
  154.4 2.7 convolution_convert_fusion
  158.1 2.7 collective-permute-start.18
  163.8 5.5 %collective-permute-done.16 = bf16[128,1024]{1,0:T(8,128)(2,1)S(1)} collective-permute-done((bf16[128,1024]{1,0:T(8,128)(2,1)S(1)}, bf16[128,1024]{1,0:T(8,128)(2,1)S(1)}, u32[]{:S(2)}, u32[]{:S(2)}) %collective-permute-start.16) | collective-permute-done | bytes 262176 | tf_op jit(solution)/shard_map/ppermute | solution.py:30
  170.3 2.4 collective-permute-done.17
  174.0 1.7 fusion.32
  181.0 2.7 collective-permute-start.25
  184.9 1.8 collective-permute-start.30
  186.7 4.8 %all-to-all-start.4 = ((bf16[16,64,128]{2,1,0:T(8,128)(2,1)}), bf16[16,64,128]{2,1,0:T(8,128)(2,1)S(1)}, u32[]{:S(2)}, u32[]{:S(2)}) async-start(bf16[16,64,128]{2,1,0:T(8,128)(2,1)} %bitcast.54), calls=%async_computation.4 | async-start | bytes 524288 | tf_op jit(solution)/shard_map/all_to_all | solution.py:46
  191.6 1.6 convert_add_fusion.out
  194.4 5.8 %all-to-all-done.4.grad_ref = bf16[16,64,128]{2,1,0:T(8,128)(2,1)S(1)} async-done(((bf16[16,64,128]{2,1,0:T(8,128)(2,1)}), bf16[16,64,128]{2,1,0:T(8,128)(2,1)S(1)}, u32[]{:S(2)}, u32[]{:S(2)}) %all-to-all-start.4) | async-done | bytes 262176 | tf_op jit(solution)/shard_map/all_to_all | solution.py:46
  200.1 3.5 %all-to-all-start.5 = ((bf16[4,144,1024]{2,1,0:T(8,128)(2,1)}), bf16[4,144,1024]{2,1,0:T(8,128)(2,1)S(1)}, u32[]{:S(2)}, u32[]{:S(2)}) async-start(bf16[4,144,1024]{2,1,0:T(8,128)(2,1)} %shard_map.299), calls=%async_computation.5 | async-start | bytes 2359296 | tf_op jit(solution)/shard_map/all_to_all | solution.py:46
  204.6 19.1 %shard_map.300 = (bf16[8,32,1024]{2,1,0:T(8,128)(2,1)S(1)}, bf16[256,1024]{1,0:T(8,128)(2,1)S(1)}, bf16[256,1024]{1,0:T(8,128)(2,1)S(1)}, bf16[256,1024]{1,0:T(8...) custom-call(s32[16]{0:T(128)S(1)} %stack.155.order, ...), custom_call_target="tpu_custom_call" | custom-call | flops 1000000 | bytes 100000 | tf_op jit(solution)/shard_map/pallas_call | solution.py:260
  226.1 1.8 fusion.11
  231.7 3.6 %all-to-all-start.6 = ((bf16[8,64,1024]{2,1,0:T(8,128)(2,1)}), bf16[8,64,1024]{2,1,0:T(8,128)(2,1)S(1)}, u32[]{:S(2)}, u32[]{:S(2)}) async-start(bf16[8,64,1024]{2,1,0:T(8,128)(2,1)} %shard_map.301), calls=%async_computation.6 | async-start | bytes 2097152 | tf_op jit(solution)/shard_map/all_to_all | solution.py:46
  235.3 2.0 add_convert_fusion.2
  237.4 2.2 collective-permute-start.27
  239.6 2.0 add_convert_fusion.1
  241.6 1.9 fusion.9
  243.6 1.4 collective-permute-start.32
  245.0 2.0 add_convert_fusion
  247.1 2.4 collective-permute-start.29
  250.5 3.1 collective-permute-done.32
  254.7 7.8 %all-to-all-start.7 = ((bf16[4,64,1024]{2,1,0:T(8,128)(2,1)}), bf16[4,64,1024]{2,1,0:T(8,128)(2,1)S(1)}, u32[]{:S(2)}, u32[]{:S(2)}) async-start(bf16[4,64,1024]{2,1,0:T(8,128)(2,1)} %pad_maximum_fusion.5), calls=%async_computation.7 | async-start | bytes 1048576 | tf_op jit(solution)/shard_map/all_to_all | solution.py:46
  262.5 4.0 %collective-permute-done.29 = bf16[256,1024]{1,0:T(8,128)(2,1)} collective-permute-done((bf16[256,1024]{1,0:T(8,128)(2,1)}, bf16[256,1024]{1,0:T(8,128)(2,1)}, u32[]{:S(2)}, u32[]{:S(2)}) %collective-permute-start.29) | collective-permute-done | bytes 524320 | tf_op jit(solution)/shard_map/ppermute | solution.py:34
  266.5 1.9 convert_add_fusion.3
  268.5 2.6 all-to-all-done.7
  271.3 1.5 broadcast_in_dim.8
  272.7 6.2 %all-to-all-start.8 = ((bf16[8,112,1024]{2,1,0:T(8,128)(2,1)}), bf16[8,112,1024]{2,1,0:T(8,128)(2,1)S(1)}, u32[]{:S(2)}, u32[]{:S(2)}) async-start(bf16[8,112,1024]{2,1,0:T(8,128)(2,1)} %broadcast_in_dim.8), calls=%async_computation.8 | async-start | bytes 3670016 | tf_op jit(solution)/shard_map/all_to_all | solution.py:46
  278.9 3.0 collective-permute-start.33
  282.0 21.8 %collective-permute-done.33 = bf16[128,1024]{1,0:T(8,128)(2,1)S(1)} collective-permute-done((bf16[128,1024]{1,0:T(8,128)(2,1)S(1)}, bf16[128,1024]{1,0:T(8,128)(2,1)S(1)}, u32[]{:S(2)}, u32[]{:S(2)}) %collective-permute-start.33) | collective-permute-done | bytes 262176 | tf_op jit(solution)/shard_map/ppermute | solution.py:30
  304.7 5.2 %collective-permute-start.34 = (bf16[8,112,1024]{2,1,0:T(8,128)(2,1)S(1)}, bf16[8,112,1024]{2,1,0:T(8,128)(2,1)}, u32[]{:S(2)}, u32[]{:S(2)}) collective-permute-start(bf16[8,112,1024]{2,1,0:T(8,128)(2,1)S(1)} %all-to-all-done.8.mine), channel_id=1, source_target_pairs={{0,8},{8,0},{16,24},{24,16},{32,40},{40,32},{48,56},{56,48},{64,72... | collective-permute-start | bytes 5505032 | tf_op jit(solution)/shard_map/ppermute | solution.py:30
  309.9 3.5 %collective-permute-done.34.theirs = bf16[8,112,1024]{2,1,0:T(8,128)(2,1)} collective-permute-done((bf16[8,112,1024]{2,1,0:T(8,128)(2,1)S(1)}, bf16[8,112,1024]{2,1,0:T(8,128)(2,1)}, u32[]{:S(2)}, u32[]{:S(2)}) %collective-permute-start.34) | collective-permute-done | bytes 1835040 | tf_op jit(solution)/shard_map/ppermute | solution.py:30
  317.4 4.6 %shard_map.302 = (f32[512,1024]{1,0:T(8,128)}, f32[128,4096]{1,0:T(8,128)}, f32[128,1024]{1,0:T(8,128)}, f32[128,1024]{1,0:T(8,128)}, f32[128,1024]{1,0:T(8,128)}, /*index=5*/f32[128,1024]{1,0:T(8,128)}) custom-call(s32[1]{0:T(128)} %bitcast.1.ctx, bf16[8,112,1024]{2,1,0:T(8,128)(2,1)S(1)} %all-to-all-done.8.mine, ...), custom_call_target="tpu_custom_call" | custom-call | flops 1000000 | bytes 10000000 | tf_op jit(solution)/shard_map/pallas_call | solution.py:260
  (215 shorter events, 47.4 us)
Async XLA Ops:
  0.7 14.1 %copy-start.1 = (bf16[128,4096]{1,0:T(8,128)(2,1)S(1)}, bf16[128,4096]{1,0:T(8,128)(2,1)}, u32[]{:S(2)}) copy-start(bf16[128,4096]{1,0:T(8,128)(2,1)} %w_up.1) | copy-start | bytes 3145732
  0.7 14.1 %copy-start.2 = (bf16[512,1024]{1,0:T(8,128)(2,1)S(1)}, bf16[512,1024]{1,0:T(8,128)(2,1)}, u32[]{:S(2)}) copy-start(bf16[512,1024]{1,0:T(8,128)(2,1)} %w_down.1) | copy-start | bytes 3145732
  6.1 12.6 %collective-permute-start = (bf16[128,1024]{1,0:T(8,128)(2,1)}, bf16[128,1024]{1,0:T(8,128)(2,1)S(1)}, u32[]{:S(2)}, u32[]{:S(2)}) collective-permute-start(bf16[128,1024]{1,0:T(8,128)(2,1)} %bitcast.186), channel_id=1, source_target_pairs={{0,16},{8,24},{16,0},{24,8},{32,48},{40,56},{48,32},{56,40},{64,80... | collective-permute-start | bytes 786440 | tf_op jit(solution)/shard_map/ppermute | solution.py:30
  9.7 14.1 %all-to-all-start = ((bf16[8,208,128]{2,1,0:T(8,128)(2,1)}), bf16[8,208,128]{2,1,0:T(8,128)(2,1)S(1)}, u32[]{:S(2)}, u32[]{:S(2)}) async-start(bf16[8,208,128]{2,1,0:T(8,128)(2,1)} %shard_map.296), calls=%async_computation | async-start | bytes 851968 | tf_op jit(solution)/shard_map/all_to_all | solution.py:46
  18.7 40.0 %copy-start = (bf16[256,1024]{1,0:T(8,128)(2,1)}, bf16[256,1024]{1,0:T(8,128)(2,1)S(1)}, u32[]{:S(2)}) copy-start(bf16[256,1024]{1,0:T(8,128)(2,1)S(1)} %pad_maximum_fusion.2.refs_0_) | copy-start | bytes 1572868
  23.8 50.5 %all-to-all-start.1 = ((bf16[8,192,1024]{2,1,0:T(8,128)(2,1)}), bf16[8,192,1024]{2,1,0:T(8,128)(2,1)}, u32[]{:S(2)}, u32[]{:S(2)}) async-start(bf16[8,192,1024]{2,1,0:T(8,128)(2,1)} %get-tuple-element.76), calls=%async_computation.1 | async-start | bytes 6291456 | tf_op jit(solution)/shard_map/all_to_all | solution.py:46
  28.3 13.2 %collective-permute-start.1 = (bf16[256,1024]{1,0:T(8,128)(2,1)S(1)}, bf16[256,1024]{1,0:T(8,128)(2,1)S(1)}, u32[]{:S(2)}, u32[]{:S(2)}) collective-permute-start(bf16[256,1024]{1,0:T(8,128)(2,1)S(1)} %pad_maximum_fusion.2.refs_0_), channel_id=1, source_target_pairs={{0,32},{8,40},{16,48},{24,56},{32,64},{40,72},{48,80},{56,88},{64,... | collective-permute-start | bytes 1572872 | tf_op jit(solution)/shard_map/ppermute | solution.py:34
  29.6 24.2 %collective-permute-start.2 = (bf16[256,1024]{1,0:T(8,128)(2,1)S(1)}, bf16[256,1024]{1,0:T(8,128)(2,1)S(1)}, u32[]{:S(2)}, u32[]{:S(2)}) collective-permute-start(bf16[256,1024]{1,0:T(8,128)(2,1)S(1)} %pad_maximum_fusion.2.refs_0_), channel_id=1, source_target_pairs={{0,64},{8,72},{16,80},{24,88},{32,96},{40,104},{48,112},{56,120},{... | collective-permute-start | bytes 1572872 | tf_op jit(solution)/shard_map/ppermute | solution.py:34
  32.2 24.1 %collective-permute-start.3 = (bf16[256,1024]{1,0:T(8,128)(2,1)S(1)}, bf16[256,1024]{1,0:T(8,128)(2,1)S(1)}, u32[]{:S(2)}, u32[]{:S(2)}) collective-permute-start(bf16[256,1024]{1,0:T(8,128)(2,1)S(1)} %pad_maximum_fusion.2.refs_0_), channel_id=1, source_target_pairs={{0,96},{8,104},{16,112},{24,120},{32,0},{40,8},{48,16},{56,24},{64... | collective-permute-start | bytes 1572872 | tf_op jit(solution)/shard_map/ppermute | solution.py:34
  33.4 23.4 %collective-permute-start.4 = (bf16[256,1024]{1,0:T(8,128)(2,1)S(1)}, bf16[256,1024]{1,0:T(8,128)(2,1)S(1)}, u32[]{:S(2)}, u32[]{:S(2)}) collective-permute-start(bf16[256,1024]{1,0:T(8,128)(2,1)S(1)} %pad_maximum_fusion.2.refs_0_), channel_id=1, source_target_pairs={{0,8},{8,0},{16,24},{24,16},{32,40},{40,32},{48,56},{56,48},{64,72... | collective-permute-start | bytes 1572872 | tf_op jit(solution)/shard_map/ppermute | solution.py:30
  41.5 31.2 %copy-start.5 = (bf16[256,1024]{1,0:T(8,128)(2,1)}, bf16[256,1024]{1,0:T(8,128)(2,1)S(1)}, u32[]{:S(2)}) copy-start(bf16[256,1024]{1,0:T(8,128)(2,1)S(1)} %collective-permute-done.1.refs_1_) | copy-start | bytes 1572868
  41.5 15.3 %collective-permute-start.5 = (bf16[256,1024]{1,0:T(8,128)(2,1)S(1)}, bf16[256,1024]{1,0:T(8,128)(2,1)}, u32[]{:S(2)}, u32[]{:S(2)}) collective-permute-start(bf16[256,1024]{1,0:T(8,128)(2,1)S(1)} %collective-permute-done.1.refs_1_), channel_id=1, source_target_pairs={{0,8},{8,0},{16,24},{24,16},{32,40},{40,32},{48,56},{56,48},{64,72... | collective-permute-start | bytes 1572872 | tf_op jit(solution)/shard_map/ppermute | solution.py:30
  53.9 18.9 %copy-start.6 = (bf16[256,1024]{1,0:T(8,128)(2,1)}, bf16[256,1024]{1,0:T(8,128)(2,1)S(1)}, u32[]{:S(2)}) copy-start(bf16[256,1024]{1,0:T(8,128)(2,1)S(1)} %collective-permute-done.2.refs_2_) | copy-start | bytes 1572868
  53.9 4.2 %collective-permute-start.6 = (bf16[256,1024]{1,0:T(8,128)(2,1)S(1)}, bf16[256,1024]{1,0:T(8,128)(2,1)}, u32[]{:S(2)}, u32[]{:S(2)}) collective-permute-start(bf16[256,1024]{1,0:T(8,128)(2,1)S(1)} %collective-permute-done.2.refs_2_), channel_id=1, source_target_pairs={{0,8},{8,0},{16,24},{24,16},{32,40},{40,32},{48,56},{56,48},{64,72... | collective-permute-start | bytes 1572872 | tf_op jit(solution)/shard_map/ppermute | solution.py:30
  56.4 2.4 collective-permute-start.7
  74.3 15.3 %copy-start.9 = (bf16[192,1024]{1,0:T(8,128)(2,1)}, bf16[192,1024]{1,0:T(8,128)(2,1)S(1)}, u32[]{:S(2)}) copy-start(bf16[192,1024]{1,0:T(8,128)(2,1)S(1)} %get-tuple-element.89.refs_8_) | copy-start | bytes 1179652
  75.8 18.6 %collective-permute-start.8 = (bf16[512,1024]{1,0:T(8,128)(2,1)S(1)}, bf16[512,1024]{1,0:T(8,128)(2,1)S(1)}, u32[]{:S(2)}, u32[]{:S(2)}) collective-permute-start(bf16[512,1024]{1,0:T(8,128)(2,1)S(1)} %bitcast.174), channel_id=1, source_target_pairs={{0,8},{8,0},{16,24},{24,16},{32,40},{40,32},{48,56},{56,48},{64,72... | collective-permute-start | bytes 3145736 | tf_op jit(solution)/shard_map/ppermute | solution.py:30
  76.2 13.4 %all-to-all-start.2 = ((bf16[16,64,128]{2,1,0:T(8,128)(2,1)}), bf16[16,64,128]{2,1,0:T(8,128)(2,1)S(1)}, u32[]{:S(2)}, u32[]{:S(2)}) async-start(bf16[16,64,128]{2,1,0:T(8,128)(2,1)} %get-tuple-element.78), calls=%async_computation.2 | async-start | bytes 524288 | tf_op jit(solution)/shard_map/all_to_all | solution.py:46
  89.6 30.2 %all-to-all-start.3 = ((bf16[8,128,1024]{2,1,0:T(8,128)(2,1)}), bf16[8,128,1024]{2,1,0:T(8,128)(2,1)}, u32[]{:S(2)}, u32[]{:S(2)}) async-start(bf16[8,128,1024]{2,1,0:T(8,128)(2,1)} %get-tuple-element.81), calls=%async_computation.3 | async-start | bytes 4194304 | tf_op jit(solution)/shard_map/all_to_all | solution.py:46
  95.8 10.7 %copy-start.27 = (bf16[128,1024]{1,0:T(8,128)(2,1)}, bf16[128,1024]{1,0:T(8,128)(2,1)S(1)}, u32[]{:S(2)}) copy-start(bf16[128,1024]{1,0:T(8,128)(2,1)S(1)} %fusion.27) | copy-start | bytes 786436
  95.8 6.7 %collective-permute-start.9 = (bf16[128,1024]{1,0:T(8,128)(2,1)S(1)}, bf16[128,1024]{1,0:T(8,128)(2,1)S(1)}, u32[]{:S(2)}, u32[]{:S(2)}) collective-permute-start(bf16[128,1024]{1,0:T(8,128)(2,1)S(1)} %fusion.27), channel_id=1, source_target_pairs={{0,32},{8,40},{16,48},{24,56},{32,0},{40,8},{48,16},{56,24},{64,96... | collective-permute-start | bytes 786440 | tf_op jit(solution)/shard_map/ppermute | solution.py:30
  102.5 3.9 %collective-permute-start.10 = (bf16[256,1024]{1,0:T(8,128)(2,1)S(1)}, bf16[256,1024]{1,0:T(8,128)(2,1)S(1)}, u32[]{:S(2)}, u32[]{:S(2)}) collective-permute-start(bf16[256,1024]{1,0:T(8,128)(2,1)S(1)} %pad_maximum_fusion.3), channel_id=1, source_target_pairs={{0,8},{8,0},{16,24},{24,16},{32,40},{40,32},{48,56},{56,48},{64,72... | collective-permute-start | bytes 1572872 | tf_op jit(solution)/shard_map/ppermute | solution.py:30
  106.5 4.9 %copy-start.37 = (bf16[256,1024]{1,0:T(8,128)(2,1)}, bf16[256,1024]{1,0:T(8,128)(2,1)S(1)}, u32[]{:S(2)}) copy-start(bf16[256,1024]{1,0:T(8,128)(2,1)S(1)} %collective-permute-done.10) | copy-start | bytes 1572868
  123.1 3.8 %collective-permute-start.11 = (bf16[256,1024]{1,0:T(8,128)(2,1)S(1)}, bf16[256,1024]{1,0:T(8,128)(2,1)S(1)}, u32[]{:S(2)}, u32[]{:S(2)}) collective-permute-start(bf16[256,1024]{1,0:T(8,128)(2,1)S(1)} %slice.306), channel_id=1, source_target_pairs={{0,8},{8,0},{16,24},{24,16},{32,40},{40,32},{48,56},{56,48},{64,72... | collective-permute-start | bytes 1572872 | tf_op jit(solution)/shard_map/ppermute | solution.py:30
  127.0 8.4 %copy-start.15 = (bf16[1,128,1024]{2,1,0:T(8,128)(2,1)S(1)}, bf16[1,128,1024]{2,1,0:T(8,128)(2,1)}, u32[]{:S(2)}) copy-start(bf16[1,128,1024]{2,1,0:T(8,128)(2,1)} %param.33) | copy-start | bytes 786436
  127.1 7.8 %collective-permute-start.12 = (bf16[128,1024]{1,0:T(8,128)(2,1)S(1)}, bf16[128,1024]{1,0:T(8,128)(2,1)S(1)}, u32[]{:S(2)}, u32[]{:S(2)}) collective-permute-start(bf16[128,1024]{1,0:T(8,128)(2,1)S(1)} %slice.309), channel_id=1, source_target_pairs={{0,32},{8,40},{16,48},{24,56},{32,0},{40,8},{48,16},{56,24},{64,96... | collective-permute-start | bytes 786440 | tf_op jit(solution)/shard_map/ppermute | solution.py:30
  135.2 11.2 %copy-start.42 = (f32[512,1024]{1,0:T(8,128)S(1)}, f32[512,1024]{1,0:T(8,128)}, u32[]{:S(2)}) copy-start(f32[512,1024]{1,0:T(8,128)} %get-tuple-element.185) | copy-start | bytes 6291460
  135.9 6.7 %collective-permute-start.13 = (bf16[128,1024]{1,0:T(8,128)(2,1)S(1)}, bf16[128,1024]{1,0:T(8,128)(2,1)S(1)}, u32[]{:S(2)}, u32[]{:S(2)}) collective-permute-start(bf16[128,1024]{1,0:T(8,128)(2,1)S(1)} %get-tuple-element.137), channel_id=1, source_target_pairs={{0,32},{8,40},{16,48},{24,56},{32,0},{40,8},{48,16},{56,24},{64,96... | collective-permute-start | bytes 786440 | tf_op jit(solution)/shard_map/ppermute | solution.py:30
  142.6 3.7 %collective-permute-start.14 = (bf16[256,1024]{1,0:T(8,128)(2,1)S(1)}, bf16[256,1024]{1,0:T(8,128)(2,1)S(1)}, u32[]{:S(2)}, u32[]{:S(2)}) collective-permute-start(bf16[256,1024]{1,0:T(8,128)(2,1)S(1)} %pad_maximum_fusion.4), channel_id=1, source_target_pairs={{0,8},{8,0},{16,24},{24,16},{32,40},{40,32},{48,56},{56,48},{64,72... | collective-permute-start | bytes 1572872 | tf_op jit(solution)/shard_map/ppermute | solution.py:30
  146.4 4.8 %copy-start.39 = (bf16[256,1024]{1,0:T(8,128)(2,1)}, bf16[256,1024]{1,0:T(8,128)(2,1)S(1)}, u32[]{:S(2)}) copy-start(bf16[256,1024]{1,0:T(8,128)(2,1)S(1)} %collective-permute-done.14) | copy-start | bytes 1572868
  146.4 4.8 %copy-start.23 = (bf16[8,128,1024]{2,1,0:T(8,128)(2,1)S(1)}, bf16[8,128,1024]{2,1,0:T(8,128)(2,1)}, u32[]{:S(2)}) copy-start(bf16[8,128,1024]{2,1,0:T(8,128)(2,1)} %copy-done.22) | copy-start | bytes 6291460
  153.9 6.9 %collective-permute-start.15 = (bf16[256,1024]{1,0:T(8,128)(2,1)S(1)}, bf16[256,1024]{1,0:T(8,128)(2,1)}, u32[]{:S(2)}, u32[]{:S(2)}) collective-permute-start(bf16[256,1024]{1,0:T(8,128)(2,1)S(1)} %slice.305), channel_id=1, source_target_pairs={{0,8},{8,0},{16,24},{24,16},{32,40},{40,32},{48,56},{56,48},{64,72... | collective-permute-start | bytes 1572872 | tf_op jit(solution)/shard_map/ppermute | solution.py:30
  157.1 5.0 %copy-start.21 = (bf16[1024,1024]{1,0:T(8,128)(2,1)}, bf16[1024,1024]{1,0:T(8,128)(2,1)S(1)}, u32[]{:S(2)}) copy-start(bf16[1024,1024]{1,0:T(8,128)(2,1)S(1)} %convolution_convert_fusion) | copy-start | bytes 6291460
  158.0 4.4 %copy-start.28 = (bf16[128,1024]{1,0:T(8,128)(2,1)S(1)}, bf16[128,1024]{1,0:T(8,128)(2,1)}, u32[]{:S(2)}) copy-start(bf16[128,1024]{1,0:T(8,128)(2,1)} %copy-done.27) | copy-start | bytes 786436
  158.0 4.4 %copy-start.36 = (bf16[128,1024]{1,0:T(8,128)(2,1)S(1)}, bf16[128,1024]{1,0:T(8,128)(2,1)}, u32[]{:S(2)}) copy-start(bf16[128,1024]{1,0:T(8,128)(2,1)} %copy-done.35) | copy-start | bytes 786436
  158.1 4.4 %copy-start.38 = (bf16[256,1024]{1,0:T(8,128)(2,1)S(1)}, bf16[256,1024]{1,0:T(8,128)(2,1)}, u32[]{:S(2)}) copy-start(bf16[256,1024]{1,0:T(8,128)(2,1)} %copy-done.37) | copy-start | bytes 1572868
  158.1 4.4 %copy-start.41 = (bf16[512,1024]{1,0:T(8,128)(2,1)S(1)}, bf16[512,1024]{1,0:T(8,128)(2,1)}, u32[]{:S(2)}) copy-start(bf16[512,1024]{1,0:T(8,128)(2,1)} %copy-done.40) | copy-start | bytes 3145732
  158.1 14.7 %collective-permute-start.17 = (bf16[2,128,1024]{2,1,0:T(8,128)(2,1)S(1)}, bf16[2,128,1024]{2,1,0:T(8,128)(2,1)S(1)}, u32[]{:S(2)}, u32[]{:S(2)}) collective-permute-start(bf16[2,128,1024]{2,1,0:T(8,128)(2,1)S(1)} %get-tuple-element.147), channel_id=1, source_target_pairs={{0,2},{1,3},{2,4},{3,5},{4,6},{5,7},{6,0},{7,1},{8,10},{9,11},{10,... | collective-permute-start | bytes 1572872 | tf_op jit(solution)/shard_map/ppermute | solution.py:38
  158.1 14.6 %collective-permute-start.18 = (bf16[2,128,1024]{2,1,0:T(8,128)(2,1)S(1)}, bf16[2,128,1024]{2,1,0:T(8,128)(2,1)S(1)}, u32[]{:S(2)}, u32[]{:S(2)}) collective-permute-start(bf16[2,128,1024]{2,1,0:T(8,128)(2,1)S(1)} %get-tuple-element.146), channel_id=1, source_target_pairs={{0,6},{1,7},{2,0},{3,1},{4,2},{5,3},{6,4},{7,5},{8,14},{9,15},{10,... | collective-permute-start | bytes 1572872 | tf_op jit(solution)/shard_map/ppermute | solution.py:38
  162.1 7.2 %collective-permute-start.16 = (bf16[128,1024]{1,0:T(8,128)(2,1)S(1)}, bf16[128,1024]{1,0:T(8,128)(2,1)S(1)}, u32[]{:S(2)}, u32[]{:S(2)}) collective-permute-start(bf16[128,1024]{1,0:T(8,128)(2,1)S(1)} %slice.308), channel_id=1, source_target_pairs={{0,32},{8,40},{16,48},{24,56},{32,0},{40,8},{48,16},{56,24},{64,96... | collective-permute-start | bytes 786440 | tf_op jit(solution)/shard_map/ppermute | solution.py:30
  163.8 16.0 %copy-start.20 = (bf16[1024,1024]{1,0:T(8,128)(2,1)}, bf16[1024,1024]{1,0:T(8,128)(2,1)S(1)}, u32[]{:S(2)}) copy-start(bf16[1024,1024]{1,0:T(8,128)(2,1)S(1)} %convolution_convert_fusion.1) | copy-start | bytes 6291460
  178.8 12.7 %collective-permute-start.19 = (bf16[8,64,1024]{2,1,0:T(8,128)(2,1)}, bf16[8,64,1024]{2,1,0:T(8,128)(2,1)}, u32[]{:S(2)}, u32[]{:S(2)}) collective-permute-start(bf16[8,64,1024]{2,1,0:T(8,128)(2,1)} %dynamic-slice_bitcast_fusion), channel_id=1, source_target_pairs={{0,8},{8,0},{16,24},{24,16},{32,40},{40,32},{48,56},{56,48},{64,72... | collective-permute-start | bytes 3145736 | tf_op jit(solution)/shard_map/ppermute | solution.py:30
  181.0 44.5 %collective-permute-start.24 = (bf16[2,128,1024]{2,1,0:T(8,128)(2,1)}, bf16[2,128,1024]{2,1,0:T(8,128)(2,1)}, u32[]{:S(2)}, u32[]{:S(2)}) collective-permute-start(bf16[2,128,1024]{2,1,0:T(8,128)(2,1)} %get-tuple-element.150), channel_id=1, source_target_pairs={{0,2},{1,3},{2,4},{3,5},{4,6},{5,7},{6,0},{7,1},{8,10},{9,11},{10,... | collective-permute-start | bytes 1572872 | tf_op jit(solution)/shard_map/ppermute | solution.py:38
  181.0 44.5 %collective-permute-start.25 = (bf16[2,128,1024]{2,1,0:T(8,128)(2,1)}, bf16[2,128,1024]{2,1,0:T(8,128)(2,1)}, u32[]{:S(2)}, u32[]{:S(2)}) collective-permute-start(bf16[2,128,1024]{2,1,0:T(8,128)(2,1)} %get-tuple-element.149), channel_id=1, source_target_pairs={{0,6},{1,7},{2,0},{3,1},{4,2},{5,3},{6,4},{7,5},{8,14},{9,15},{10,... | collective-permute-start | bytes 1572872 | tf_op jit(solution)/shard_map/ppermute | solution.py:38
  183.7 42.5 %collective-permute-start.26 = (bf16[2,128,1024]{2,1,0:T(8,128)(2,1)}, bf16[2,128,1024]{2,1,0:T(8,128)(2,1)}, u32[]{:S(2)}, u32[]{:S(2)}) collective-permute-start(bf16[2,128,1024]{2,1,0:T(8,128)(2,1)} %get-tuple-element.148), channel_id=1, source_target_pairs={{0,4},{1,5},{2,6},{3,7},{4,0},{5,1},{6,2},{7,3},{8,12},{9,13},{10,... | collective-permute-start | bytes 1572872 | tf_op jit(solution)/shard_map/ppermute | solution.py:38
  184.9 41.2 %collective-permute-start.30 = (bf16[2,128,1024]{2,1,0:T(8,128)(2,1)}, bf16[2,128,1024]{2,1,0:T(8,128)(2,1)}, u32[]{:S(2)}, u32[]{:S(2)}) collective-permute-start(bf16[2,128,1024]{2,1,0:T(8,128)(2,1)} %get-tuple-element.145), channel_id=1, source_target_pairs={{0,4},{1,5},{2,6},{3,7},{4,0},{5,1},{6,2},{7,3},{8,12},{9,13},{10,... | collective-permute-start | bytes 1572872 | tf_op jit(solution)/shard_map/ppermute | solution.py:38
  186.7 13.5 %all-to-all-start.4 = ((bf16[16,64,128]{2,1,0:T(8,128)(2,1)}), bf16[16,64,128]{2,1,0:T(8,128)(2,1)S(1)}, u32[]{:S(2)}, u32[]{:S(2)}) async-start(bf16[16,64,128]{2,1,0:T(8,128)(2,1)} %bitcast.54), calls=%async_computation.4 | async-start | bytes 524288 | tf_op jit(solution)/shard_map/all_to_all | solution.py:46
  200.1 29.4 %all-to-all-start.5 = ((bf16[4,144,1024]{2,1,0:T(8,128)(2,1)}), bf16[4,144,1024]{2,1,0:T(8,128)(2,1)S(1)}, u32[]{:S(2)}, u32[]{:S(2)}) async-start(bf16[4,144,1024]{2,1,0:T(8,128)(2,1)} %shard_map.299), calls=%async_computation.5 | async-start | bytes 2359296 | tf_op jit(solution)/shard_map/all_to_all | solution.py:46
  224.5 10.7 %collective-permute-start.20 = (bf16[256,1024]{1,0:T(8,128)(2,1)}, bf16[256,1024]{1,0:T(8,128)(2,1)}, u32[]{:S(2)}, u32[]{:S(2)}) collective-permute-start(bf16[256,1024]{1,0:T(8,128)(2,1)} %get-tuple-element.94), channel_id=1, source_target_pairs={{0,8},{8,0},{16,24},{24,16},{32,40},{40,32},{48,56},{56,48},{64,72... | collective-permute-start | bytes 1572872 | tf_op jit(solution)/shard_map/ppermute | solution.py:30
  225.5 9.8 %collective-permute-start.21 = (bf16[256,1024]{1,0:T(8,128)(2,1)}, bf16[256,1024]{1,0:T(8,128)(2,1)}, u32[]{:S(2)}, u32[]{:S(2)}) collective-permute-start(bf16[256,1024]{1,0:T(8,128)(2,1)} %get-tuple-element.95), channel_id=1, source_target_pairs={{0,8},{8,0},{16,24},{24,16},{32,40},{40,32},{48,56},{56,48},{64,72... | collective-permute-start | bytes 1572872 | tf_op jit(solution)/shard_map/ppermute | solution.py:30
  225.5 9.8 %collective-permute-start.22 = (bf16[256,1024]{1,0:T(8,128)(2,1)}, bf16[256,1024]{1,0:T(8,128)(2,1)}, u32[]{:S(2)}, u32[]{:S(2)}) collective-permute-start(bf16[256,1024]{1,0:T(8,128)(2,1)} %get-tuple-element.96), channel_id=1, source_target_pairs={{0,8},{8,0},{16,24},{24,16},{32,40},{40,32},{48,56},{56,48},{64,72... | collective-permute-start | bytes 1572872 | tf_op jit(solution)/shard_map/ppermute | solution.py:30
  226.0 9.3 %collective-permute-start.23 = (bf16[256,1024]{1,0:T(8,128)(2,1)}, bf16[256,1024]{1,0:T(8,128)(2,1)}, u32[]{:S(2)}, u32[]{:S(2)}) collective-permute-start(bf16[256,1024]{1,0:T(8,128)(2,1)} %get-tuple-element.97), channel_id=1, source_target_pairs={{0,8},{8,0},{16,24},{24,16},{32,40},{40,32},{48,56},{56,48},{64,72... | collective-permute-start | bytes 1572872 | tf_op jit(solution)/shard_map/ppermute | solution.py:30
  229.0 20.5 %collective-permute-start.31 = (bf16[128,1024]{1,0:T(8,128)(2,1)S(1)}, bf16[128,1024]{1,0:T(8,128)(2,1)}, u32[]{:S(2)}, u32[]{:S(2)}) collective-permute-start(bf16[128,1024]{1,0:T(8,128)(2,1)S(1)} %fusion.30), channel_id=1, source_target_pairs={{0,1},{1,0},{2,3},{3,2},{4,5},{5,4},{6,7},{7,6},{8,9},{9,8},{10,11... | collective-permute-start | bytes 786440 | tf_op jit(solution)/shard_map/ppermute | solution.py:42
  231.7 22.8 %all-to-all-start.6 = ((bf16[8,64,1024]{2,1,0:T(8,128)(2,1)}), bf16[8,64,1024]{2,1,0:T(8,128)(2,1)S(1)}, u32[]{:S(2)}, u32[]{:S(2)}) async-start(bf16[8,64,1024]{2,1,0:T(8,128)(2,1)} %shard_map.301), calls=%async_computation.6 | async-start | bytes 2097152 | tf_op jit(solution)/shard_map/all_to_all | solution.py:46
  237.4 25.2 %collective-permute-start.27 = (bf16[256,1024]{1,0:T(8,128)(2,1)}, bf16[256,1024]{1,0:T(8,128)(2,1)}, u32[]{:S(2)}, u32[]{:S(2)}) collective-permute-start(bf16[256,1024]{1,0:T(8,128)(2,1)} %add_convert_fusion.2), channel_id=1, source_target_pairs={{0,96},{8,104},{16,112},{24,120},{32,0},{40,8},{48,16},{56,24},{64... | collective-permute-start | bytes 1572872 | tf_op jit(solution)/shard_map/ppermute | solution.py:34
  241.6 7.8 %copy-start.17 = (f32[2,128,1024]{2,1,0:T(8,128)S(1)}, f32[2,128,1024]{2,1,0:T(8,128)}, u32[]{:S(2)}) copy-start(f32[2,128,1024]{2,1,0:T(8,128)} %copy-done.16) | copy-start | bytes 3145732
  241.6 20.9 %collective-permute-start.28 = (bf16[256,1024]{1,0:T(8,128)(2,1)}, bf16[256,1024]{1,0:T(8,128)(2,1)}, u32[]{:S(2)}, u32[]{:S(2)}) collective-permute-start(bf16[256,1024]{1,0:T(8,128)(2,1)} %add_convert_fusion.1), channel_id=1, source_target_pairs={{0,32},{8,40},{16,48},{24,56},{32,64},{40,72},{48,80},{56,88},{64,... | collective-permute-start | bytes 1572872 | tf_op jit(solution)/shard_map/ppermute | solution.py:34
  243.6 10.0 %collective-permute-start.32 = (bf16[128,1024]{1,0:T(8,128)(2,1)S(1)}, bf16[128,1024]{1,0:T(8,128)(2,1)S(1)}, u32[]{:S(2)}, u32[]{:S(2)}) collective-permute-start(bf16[128,1024]{1,0:T(8,128)(2,1)S(1)} %fusion.31), channel_id=1, source_target_pairs={{0,1},{1,0},{2,3},{3,2},{4,5},{5,4},{6,7},{7,6},{8,9},{9,8},{10,11... | collective-permute-start | bytes 786440 | tf_op jit(solution)/shard_map/ppermute | solution.py:42
  247.1 19.4 %collective-permute-start.29 = (bf16[256,1024]{1,0:T(8,128)(2,1)}, bf16[256,1024]{1,0:T(8,128)(2,1)}, u32[]{:S(2)}, u32[]{:S(2)}) collective-permute-start(bf16[256,1024]{1,0:T(8,128)(2,1)} %add_convert_fusion), channel_id=1, source_target_pairs={{0,64},{8,72},{16,80},{24,88},{32,96},{40,104},{48,112},{56,120},{... | collective-permute-start | bytes 1572872 | tf_op jit(solution)/shard_map/ppermute | solution.py:34
  254.7 16.4 %all-to-all-start.7 = ((bf16[4,64,1024]{2,1,0:T(8,128)(2,1)}), bf16[4,64,1024]{2,1,0:T(8,128)(2,1)S(1)}, u32[]{:S(2)}, u32[]{:S(2)}) async-start(bf16[4,64,1024]{2,1,0:T(8,128)(2,1)} %pad_maximum_fusion.5), calls=%async_computation.7 | async-start | bytes 1048576 | tf_op jit(solution)/shard_map/all_to_all | solution.py:46
  272.7 31.1 %copy-start.24 = (f32[128,1024]{1,0:T(8,128)S(1)}, f32[128,1024]{1,0:T(8,128)}, u32[]{:S(2)}) copy-start(f32[128,1024]{1,0:T(8,128)} %get-tuple-element.140) | copy-start | bytes 1572868
  272.7 31.9 %all-to-all-start.8 = ((bf16[8,112,1024]{2,1,0:T(8,128)(2,1)}), bf16[8,112,1024]{2,1,0:T(8,128)(2,1)S(1)}, u32[]{:S(2)}, u32[]{:S(2)}) async-start(bf16[8,112,1024]{2,1,0:T(8,128)(2,1)} %broadcast_in_dim.8), calls=%async_computation.8 | async-start | bytes 3670016 | tf_op jit(solution)/shard_map/all_to_all | solution.py:46
  278.9 24.8 %collective-permute-start.33 = (bf16[128,1024]{1,0:T(8,128)(2,1)S(1)}, bf16[128,1024]{1,0:T(8,128)(2,1)S(1)}, u32[]{:S(2)}, u32[]{:S(2)}) collective-permute-start(bf16[128,1024]{1,0:T(8,128)(2,1)S(1)} %slice.307), channel_id=1, source_target_pairs={{0,16},{8,24},{16,0},{24,8},{32,48},{40,56},{48,32},{56,40},{64,80... | collective-permute-start | bytes 786440 | tf_op jit(solution)/shard_map/ppermute | solution.py:30
  304.7 8.8 %collective-permute-start.34 = (bf16[8,112,1024]{2,1,0:T(8,128)(2,1)S(1)}, bf16[8,112,1024]{2,1,0:T(8,128)(2,1)}, u32[]{:S(2)}, u32[]{:S(2)}) collective-permute-start(bf16[8,112,1024]{2,1,0:T(8,128)(2,1)S(1)} %all-to-all-done.8.mine), channel_id=1, source_target_pairs={{0,8},{8,0},{16,24},{24,16},{32,40},{40,32},{48,56},{56,48},{64,72... | collective-permute-start | bytes 5505032 | tf_op jit(solution)/shard_map/ppermute | solution.py:30
  (23 other events, 42.7 us)
where the time goes:
time: 324 us; the launch traced here: 322 us
  waiting for transfers between devices  110 us (34%)
  starting transfers between devices  96.6 us (30%)
  Pallas kernels  43.9 us (14%)
  local copies, waits for them, and re-layouts  25.9 us (8%)
  other arithmetic  23.4 us (7%)
  matrix products  20.4 us (6%)
    ppermute x21, waiting for transfers between devices, swap(): return lax.ppermute(block, 'ctx', [(i, i ^ bit) for i in range(16)])  55.8 us
    all_to_all x9, starting transfers between devices, exchange(): lax.all_to_all(blocks, axis, 0, 0, axis_index_groups=groups, tiled=True)  44.4 us
    pallas_call x7, Pallas kernels, call(): pl.pallas_call(kernel, out_shape=[jax.ShapeDtypeStruct(shape, dtype) for...  43.9 us
    ppermute x21, starting transfers between devices, swap(): return lax.ppermute(block, 'ctx', [(i, i ^ bit) for i in range(16)])  32.2 us
    all_to_all x9, waiting for transfers between devices, exchange(): lax.all_to_all(blocks, axis, 0, 0, axis_index_groups=groups, tiled=True)  30.5 us
    dot_general x11, matrix products, dims(): lax.dot_general(matrix, other, (((left,), (right,)), ((), ())), preferred...  20.4 us
    ppermute x6, waiting for transfers between devices, along_y(): lax.ppermute(block, 'ctx', [(i, (i + 4 * steps) % 16) for i in range(16)])  18.4 us
    unnamed x86, local copies, waits for them, and re-layouts  12.4 us
  transfers between devices with their start and end apart: 44, of which 20 were waited for; matrix products, arithmetic and copies ran while one was open for 10% of the time, Pallas kernels for 12%

commit v1 on v0

--- a/solution.py
+++ b/solution.py
@@ -101,11 +101,13 @@
     core = at & 1
     quarter = ((at >> 2) & 1) * 2 + core
     for f in range(8):
+        rows = pl.multiple_of(quarter * ROWS, ROWS)
+        early[f, 64 + ROWS :, :] = w_down[pl.ds(rows, 48), :]
+        late[f] = w_down[pl.ds(pl.multiple_of(rows + 48, 16), 80), :]
         early[f, :64, :] = w_out[pl.ds(pl.multiple_of(core * 64, 64), 64), :]
-        late[f] = w_down[pl.ds(pl.multiple_of(quarter * ROWS, ROWS), ROWS), :]
         for block in range(8):
             span = pl.ds(pl.multiple_of(block * 512 + quarter * ROWS, ROWS), ROWS)
-            early[f, 64:, block * ROWS : (block + 1) * ROWS] = w_up[:, span]
+            early[f, 64 : 64 + ROWS, block * ROWS : (block + 1) * ROWS] = w_up[:, span]
 
 
 def forward_kernel(order, *refs):
@@ -327,7 +329,7 @@
 
     early, late = call(
         weights_kernel,
-        [((8, 64 + ROWS, WIDTH), LOW), ((8, ROWS, WIDTH), LOW)],
+        [((8, 240, WIDTH), LOW), ((8, 80, WIDTH), LOW)],
         [],
         10**6,
         10**7,
@@ -380,14 +382,15 @@
     context = exchange(mixed_low, "ctx")
     out_mine = early[:, :64].reshape(512, WIDTH)
     out_theirs = swap(out_mine, CORE)
-    mat_up = early[:, 64:].reshape(WIDTH, WIDTH)
-    mat_down = exchange(after(late, context), "fsdp").reshape(WIDTH, WIDTH)
+    mat_up = early[:, 64 : 64 + ROWS].reshape(WIDTH, WIDTH)
+    late = exchange(after(late, context), "fsdp")
+    early_down = early[:, 64 + ROWS :]
     context_mine = pick(context.reshape(8, 2, HEAD, ROWS), core, 1).reshape(512, ROWS)
     context_theirs = pick(context.reshape(8, 2, HEAD, ROWS), 1 - core, 1).reshape(512, ROWS)
     context = context.reshape(WIDTH, ROWS)
 
-    def share(block):
-        block = jnp.concatenate([block, swap(block, NEAR_Y)], axis=0)
+    def share(block, ready=()):
+        block = after(jnp.concatenate([block, swap(block, NEAR_Y)], axis=0), ready)
         return jnp.concatenate([block, swap(block, CORE)], axis=0)
 
     def collect(partial):
@@ -396,7 +399,9 @@
 
     branch = dims(context_mine, out_mine, 0, 0) + dims(context_theirs, out_theirs, 0, 0) + vec_out
     first, unit_one, scale_one = norm_forward(own.astype(F32) + branch, gain_a, shift_a)
-    first_all = share(first.astype(LOW))
+    mat_up, early_down = lax.optimization_barrier((mat_up, early_down))
+    first_all = share(first.astype(LOW), (mat_up, early_down))
+    mat_down = jnp.concatenate([early_down, late], axis=1).reshape(WIDTH, WIDTH)
     hidden = dot(first_all, mat_up) + vec_up
     gate = 0.5 * (1.0 + lax.erf(hidden * (0.5**0.5)))
     slope = gate + hidden * jnp.exp(-0.5 * hidden * hidden) * 0.3989422804014327
@@ -416,9 +421,9 @@
     grad_vec_up = jnp.sum(grad_hidden.astype(F32), axis=0)
     up = dims(first_all, grad_hidden, 0, 0).astype(LOW).reshape(4, 2, ROWS, WIDTH)
     grad_first = grad_two + collect(dims(grad_hidden, mat_up, 1, 1))
-    grad_first = after(grad_first, (up, down_found[:2]))
+    grad_first = after(grad_first, up)
     grad_one, grad_gain_a, grad_shift_a = norm_backward(grad_first, unit_one, scale_one, gain_a)
-    grad_branch = grad_one.astype(LOW)
+    grad_branch = after(grad_one.astype(LOW), down_found[:2])
     grad_vec_out = jnp.sum(grad_branch.astype(F32), axis=0)
     grad_context = by_core(
         dims(out_mine, grad_branch, 1, 1).reshape(8, HEAD, ROWS),
@@ -463,6 +468,7 @@
         *parts,
         own_weight,
     )
+    up = after(up, quarter_message)
     up_found = [along_z(pick(up, (z + k) % 4, 0), k) for k in (1, 3, 2)]
     down_found = after([*down_found[:2], after(down_found[2], grad_context)], message)
     theirs = [swap(share, CORE) for share in shares[4:]]

time: 324 us -> 316 us (0.975)
  waiting for transfers between devices: 110 us -> 93.3 us
  local copies, waits for them, and re-layouts: 25.9 us -> 34.9 us
  matrix products: 20.4 us -> 16.9 us
    all_to_all x9, waiting for transfers between devices: 30.5 us -> 20.5 us  [exchange(): lax.all_to_all(blocks, axis, 0, 0, axis_index_groups=groups, tiled=True)]
    ppermute x21, waiting for transfers between devices: 55.8 us -> 48.6 us  [swap(): return lax.ppermute(block, 'ctx', [(i, i ^ bit) for i in range(16)])]
    dot_general x11, matrix products: 20.4 us -> 16.9 us  [dims(): lax.dot_general(matrix, other, (((left,), (right,)), ((), ())), preferred...]
    slice x1 -> x2, local copies, waits for them, and re-layouts: 1.76 us -> 5.16 us  [the longest x1 3.08 us: on_device(): mat_up = early[:, 64:64 + ROWS].reshape(WIDTH, WIDTH)]
    unnamed x86 -> x97, local copies, waits for them, and re-layouts: 12.4 us -> 13.8 us
  transfers between devices with their start and end apart: 44 -> 44, of which waited for: 20 -> 20; matrix products, arithmetic and copies ran while one was open for 10% -> 13% of each run, Pallas kernels for 12% -> 12%
where the time goes in v1:
time: 316 us; the launch traced here: 314 us
  starting transfers between devices  98.8 us (31%)
  waiting for transfers between devices  93.3 us (30%)
  Pallas kernels  44 us (14%)
  local copies, waits for them, and re-layouts  34.9 us (11%)
  other arithmetic  24.7 us (8%)
  matrix products  16.9 us (5%)
    ppermute x21, waiting for transfers between devices, swap(): return lax.ppermute(block, 'ctx', [(i, i ^ bit) for i in range(16)])  48.6 us
    all_to_all x9, starting transfers between devices, exchange(): lax.all_to_all(blocks, axis, 0, 0, axis_index_groups=groups, tiled=True)  46.3 us
    pallas_call x7, Pallas kernels, call(): pl.pallas_call(kernel, out_shape=[jax.ShapeDtypeStruct(shape, dtype) for...  44 us
    ppermute x21, starting transfers between devices, swap(): return lax.ppermute(block, 'ctx', [(i, i ^ bit) for i in range(16)])  32.9 us
    all_to_all x9, waiting for transfers between devices, exchange(): lax.all_to_all(blocks, axis, 0, 0, axis_index_groups=groups, tiled=True)  20.5 us
    ppermute x6, waiting for transfers between devices, along_y(): lax.ppermute(block, 'ctx', [(i, (i + 4 * steps) % 16) for i in range(16)])  19 us
    dot_general x11, matrix products, dims(): lax.dot_general(matrix, other, (((left,), (right,)), ((), ())), preferred...  16.9 us
    unnamed x97, local copies, waits for them, and re-layouts  13.8 us
  transfers between devices with their start and end apart: 44, of which 20 were waited for; matrix products, arithmetic and copies ran while one was open for 13% of the time, Pallas kernels for 12%

profile of v1, /device:TPU:1, one launch (start us, length us, event | category | flops | bytes accessed | tf_op | source)
XLA Modules:
  0.0 314.1 jit_solution(15195609330761494732)
XLA Ops:
  0.7 1.6 concatenate.62.vectors
  6.1 3.6 %collective-permute-start = (bf16[128,1024]{1,0:T(8,128)(2,1)}, bf16[128,1024]{1,0:T(8,128)(2,1)S(1)}, u32[]{:S(2)}, u32[]{:S(2)}) collective-permute-start(bf16[128,1024]{1,0:T(8,128)(2,1)} %bitcast.190), channel_id=1, source_target_pairs={{0,16},{8,24},{16,0},{24,8},{32,48},{40,56},{48,32},{56,40},{64,80... | collective-permute-start | bytes 786440 | tf_op jit(solution)/shard_map/ppermute | solution.py:30
  9.7 5.1 %all-to-all-start = ((bf16[8,208,128]{2,1,0:T(8,128)(2,1)}), bf16[8,208,128]{2,1,0:T(8,128)(2,1)S(1)}, u32[]{:S(2)}, u32[]{:S(2)}) async-start(bf16[8,208,128]{2,1,0:T(8,128)(2,1)} %shard_map.296), calls=%async_computation | async-start | bytes 851968 | tf_op jit(solution)/shard_map/all_to_all | solution.py:46
  15.7 3.0 shard_map.297
  18.8 5.0 %all-to-all-done.refs_8_ = bf16[8,208,128]{2,1,0:T(8,128)(2,1)S(1)} async-done(((bf16[8,208,128]{2,1,0:T(8,128)(2,1)}), bf16[8,208,128]{2,1,0:T(8,128)(2,1)S(1)}, u32[]{:S(2)}, u32[]{:S(2)}) %all-to-all-start) | async-done | bytes 426016 | tf_op jit(solution)/shard_map/all_to_all | solution.py:46
  23.8 4.5 %all-to-all-start.1 = ((bf16[8,240,1024]{2,1,0:T(8,128)(2,1)}), bf16[8,240,1024]{2,1,0:T(8,128)(2,1)}, u32[]{:S(2)}, u32[]{:S(2)}) async-start(bf16[8,240,1024]{2,1,0:T(8,128)(2,1)} %get-tuple-element.81), calls=%async_computation.1 | async-start | bytes 7864320 | tf_op jit(solution)/shard_map/all_to_all | solution.py:46
  29.7 2.6 collective-permute-start.2
  33.5 2.6 collective-permute-start.4
  36.1 5.5 %collective-permute-done.1.refs_1_ = bf16[256,1024]{1,0:T(8,128)(2,1)S(1)} collective-permute-done((bf16[256,1024]{1,0:T(8,128)(2,1)S(1)}, bf16[256,1024]{1,0:T(8,128)(2,1)S(1)}, u32[]{:S(2)}, u32[]{:S(2)}) %collective-permute-start.1) | collective-permute-done | bytes 524320 | tf_op jit(solution)/shard_map/ppermute | solution.py:34
  41.6 3.5 %collective-permute-start.5 = (bf16[256,1024]{1,0:T(8,128)(2,1)S(1)}, bf16[256,1024]{1,0:T(8,128)(2,1)}, u32[]{:S(2)}, u32[]{:S(2)}) collective-permute-start(bf16[256,1024]{1,0:T(8,128)(2,1)S(1)} %collective-permute-done.1.refs_1_), channel_id=1, source_target_pairs={{0,8},{8,0},{16,24},{24,16},{32,40},{40,32},{48,56},{56,48},{64,72... | collective-permute-start | bytes 1572872 | tf_op jit(solution)/shard_map/ppermute | solution.py:30
  45.0 8.9 %collective-permute-done.2.refs_2_ = bf16[256,1024]{1,0:T(8,128)(2,1)S(1)} collective-permute-done((bf16[256,1024]{1,0:T(8,128)(2,1)S(1)}, bf16[256,1024]{1,0:T(8,128)(2,1)S(1)}, u32[]{:S(2)}, u32[]{:S(2)}) %collective-permute-start.2) | collective-permute-done | bytes 524320 | tf_op jit(solution)/shard_map/ppermute | solution.py:34
  53.9 2.5 collective-permute-start.6
  58.9 13.9 %shard_map.298 = (bf16[192,2048]{1,0:T(8,128)(2,1)}, bf16[2048,128]{1,0:T(8,128)(2,1)S(1)}, bf16[16,64,128]{2,1,0:T(8,128)(2,1)}, f32[64,2048]{1,0:T(8,128)S(1)}...) custom-call(s32[16]{0:T(128)S(1)} %stack.155.order, bf16[256,1024]{1,0:T(8,128)(2,1)S(1)} %pad_maximum_fusion.4.refs_0_, ...), custom_call_target="tpu_custom_call" | custom-call | flops 10000000000 | bytes 10000000 | tf_op jit(solution)/shard_map/pallas_call | solution.py:262
  74.4 2.4 slice.189
  78.2 6.0 %all-to-all-start.2 = ((bf16[16,64,128]{2,1,0:T(8,128)(2,1)}), bf16[16,64,128]{2,1,0:T(8,128)(2,1)S(1)}, u32[]{:S(2)}, u32[]{:S(2)}) async-start(bf16[16,64,128]{2,1,0:T(8,128)(2,1)} %get-tuple-element.83), calls=%async_computation.2 | async-start | bytes 524288 | tf_op jit(solution)/shard_map/all_to_all | solution.py:46
  84.3 8.7 %all-to-all-done.2 = bf16[16,64,128]{2,1,0:T(8,128)(2,1)S(1)} async-done(((bf16[16,64,128]{2,1,0:T(8,128)(2,1)}), bf16[16,64,128]{2,1,0:T(8,128)(2,1)S(1)}, u32[]{:S(2)}, u32[]{:S(2)}) %all-to-all-start.2) | async-done | bytes 262176 | tf_op jit(solution)/shard_map/all_to_all | solution.py:46
  92.9 3.6 %all-to-all-start.3 = ((bf16[8,80,1024]{2,1,0:T(8,128)(2,1)}), bf16[8,80,1024]{2,1,0:T(8,128)(2,1)S(1)}, u32[]{:S(2)}, u32[]{:S(2)}) async-start(bf16[8,80,1024]{2,1,0:T(8,128)(2,1)} %get-tuple-element.89), calls=%async_computation.3 | async-start | bytes 2621440 | tf_op jit(solution)/shard_map/all_to_all | solution.py:46
  96.6 1.6 fusion.65
  99.4 3.1 slice.193
  102.5 2.1 slice.194
  106.8 1.9 collective-permute-start.10
  108.7 1.9 constant_dynamic-update-slice_fusion.1
  110.5 3.5 %all-to-all-done.3 = bf16[8,80,1024]{2,1,0:T(8,128)(2,1)S(1)} async-done(((bf16[8,80,1024]{2,1,0:T(8,128)(2,1)}), bf16[8,80,1024]{2,1,0:T(8,128)(2,1)S(1)}, u32[]{:S(2)}, u32[]{:S(2)}) %all-to-all-start.3) | async-done | bytes 1310752 | tf_op jit(solution)/shard_map/all_to_all | solution.py:46
  114.1 1.5 pad_maximum_fusion
  116.7 1.5 multiply_convert_fusion
  120.5 2.0 collective-permute-start.11
  122.5 1.5 collective-permute-done.11
  124.8 7.2 %collective-permute-done.12 = bf16[128,1024]{1,0:T(8,128)(2,1)S(1)} collective-permute-done((bf16[128,1024]{1,0:T(8,128)(2,1)S(1)}, bf16[128,1024]{1,0:T(8,128)(2,1)S(1)}, u32[]{:S(2)}, u32[]{:S(2)}) %collective-permute-start.12) | collective-permute-done | bytes 262176 | tf_op jit(solution)/shard_map/ppermute | solution.py:30
  133.5 6.3 %collective-permute-done.13 = bf16[128,1024]{1,0:T(8,128)(2,1)S(1)} collective-permute-done((bf16[128,1024]{1,0:T(8,128)(2,1)S(1)}, bf16[128,1024]{1,0:T(8,128)(2,1)S(1)}, u32[]{:S(2)}, u32[]{:S(2)}) %collective-permute-start.13) | collective-permute-done | bytes 262176 | tf_op jit(solution)/shard_map/ppermute | solution.py:30
  139.9 2.2 collective-permute-start.14
  142.1 1.5 collective-permute-done.14
  143.6 2.7 convert_reduce_fusion.1
  150.2 2.8 convolution_convert_fusion
  154.0 2.7 collective-permute-start.18
  157.2 2.6 convolution_convert_fusion.1
  159.8 4.2 %collective-permute-done.16 = bf16[128,1024]{1,0:T(8,128)(2,1)S(1)} collective-permute-done((bf16[128,1024]{1,0:T(8,128)(2,1)S(1)}, bf16[128,1024]{1,0:T(8,128)(2,1)S(1)}, u32[]{:S(2)}, u32[]{:S(2)}) %collective-permute-start.16) | collective-permute-done | bytes 262176 | tf_op jit(solution)/shard_map/ppermute | solution.py:30
  166.4 2.2 collective-permute-done.17
  169.0 1.7 fusion.33
  175.5 3.6 %all-to-all-start.4 = ((bf16[16,64,128]{2,1,0:T(8,128)(2,1)}), bf16[16,64,128]{2,1,0:T(8,128)(2,1)S(1)}, u32[]{:S(2)}, u32[]{:S(2)}) async-start(bf16[16,64,128]{2,1,0:T(8,128)(2,1)} %bitcast.54), calls=%async_computation.4 | async-start | bytes 524288 | tf_op jit(solution)/shard_map/all_to_all | solution.py:46
  179.3 1.6 convert_add_fusion.out
  184.2 2.1 collective-permute-start.24
  187.9 5.6 %all-to-all-start.5 = ((bf16[4,144,1024]{2,1,0:T(8,128)(2,1)}), bf16[4,144,1024]{2,1,0:T(8,128)(2,1)S(1)}, u32[]{:S(2)}, u32[]{:S(2)}) async-start(bf16[4,144,1024]{2,1,0:T(8,128)(2,1)} %shard_map.299), calls=%async_computation.5 | async-start | bytes 2359296 | tf_op jit(solution)/shard_map/all_to_all | solution.py:46
  195.6 19.1 %shard_map.300 = (bf16[8,32,1024]{2,1,0:T(8,128)(2,1)S(1)}, bf16[256,1024]{1,0:T(8,128)(2,1)S(1)}, bf16[256,1024]{1,0:T(8,128)(2,1)S(1)}, bf16[256,1024]{1,0:T(8...) custom-call(s32[16]{0:T(128)S(1)} %stack.155.order, ...), custom_call_target="tpu_custom_call" | custom-call | flops 1000000 | bytes 100000 | tf_op jit(solution)/shard_map/pallas_call | solution.py:262
  217.3 1.8 fusion.11
  223.1 4.3 %all-to-all-start.6 = ((bf16[8,64,1024]{2,1,0:T(8,128)(2,1)}), bf16[8,64,1024]{2,1,0:T(8,128)(2,1)S(1)}, u32[]{:S(2)}, u32[]{:S(2)}) async-start(bf16[8,64,1024]{2,1,0:T(8,128)(2,1)} %shard_map.301), calls=%async_computation.6 | async-start | bytes 2097152 | tf_op jit(solution)/shard_map/all_to_all | solution.py:46
  227.4 2.0 add_convert_fusion.2
  229.4 3.0 collective-permute-start.27
  232.4 2.0 add_convert_fusion.1
  234.4 1.9 fusion.9
  236.4 1.5 collective-permute-start.32
  238.0 2.0 add_convert_fusion
  240.0 1.6 collective-permute-start.29
  242.6 3.1 collective-permute-done.32
  246.8 6.9 %all-to-all-start.7 = ((bf16[4,64,1024]{2,1,0:T(8,128)(2,1)}), bf16[4,64,1024]{2,1,0:T(8,128)(2,1)S(1)}, u32[]{:S(2)}, u32[]{:S(2)}) async-start(bf16[4,64,1024]{2,1,0:T(8,128)(2,1)} %pad_maximum_fusion.7), calls=%async_computation.7 | async-start | bytes 1048576 | tf_op jit(solution)/shard_map/all_to_all | solution.py:46
  253.8 4.6 %collective-permute-done.29 = bf16[256,1024]{1,0:T(8,128)(2,1)} collective-permute-done((bf16[256,1024]{1,0:T(8,128)(2,1)}, bf16[256,1024]{1,0:T(8,128)(2,1)}, u32[]{:S(2)}, u32[]{:S(2)}) %collective-permute-start.29) | collective-permute-done | bytes 524320 | tf_op jit(solution)/shard_map/ppermute | solution.py:34
  258.4 1.9 convert_add_fusion.3
  260.4 2.2 all-to-all-done.7
  262.8 1.5 broadcast_in_dim.8
  264.3 6.7 %all-to-all-start.8 = ((bf16[8,112,1024]{2,1,0:T(8,128)(2,1)}), bf16[8,112,1024]{2,1,0:T(8,128)(2,1)S(1)}, u32[]{:S(2)}, u32[]{:S(2)}) async-start(bf16[8,112,1024]{2,1,0:T(8,128)(2,1)} %broadcast_in_dim.8), calls=%async_computation.8 | async-start | bytes 3670016 | tf_op jit(solution)/shard_map/all_to_all | solution.py:46
  271.0 3.0 collective-permute-start.33
  274.1 21.7 %collective-permute-done.33 = bf16[128,1024]{1,0:T(8,128)(2,1)S(1)} collective-permute-done((bf16[128,1024]{1,0:T(8,128)(2,1)S(1)}, bf16[128,1024]{1,0:T(8,128)(2,1)S(1)}, u32[]{:S(2)}, u32[]{:S(2)}) %collective-permute-start.33) | collective-permute-done | bytes 262176 | tf_op jit(solution)/shard_map/ppermute | solution.py:30
  296.6 5.4 %collective-permute-start.34 = (bf16[8,112,1024]{2,1,0:T(8,128)(2,1)S(1)}, bf16[8,112,1024]{2,1,0:T(8,128)(2,1)}, u32[]{:S(2)}, u32[]{:S(2)}) collective-permute-start(bf16[8,112,1024]{2,1,0:T(8,128)(2,1)S(1)} %all-to-all-done.8.mine), channel_id=1, source_target_pairs={{0,8},{8,0},{16,24},{24,16},{32,40},{40,32},{48,56},{56,48},{64,72... | collective-permute-start | bytes 5505032 | tf_op jit(solution)/shard_map/ppermute | solution.py:30
  302.0 3.5 %collective-permute-done.34.theirs = bf16[8,112,1024]{2,1,0:T(8,128)(2,1)} collective-permute-done((bf16[8,112,1024]{2,1,0:T(8,128)(2,1)S(1)}, bf16[8,112,1024]{2,1,0:T(8,128)(2,1)}, u32[]{:S(2)}, u32[]{:S(2)}) %collective-permute-start.34) | collective-permute-done | bytes 1835040 | tf_op jit(solution)/shard_map/ppermute | solution.py:30
  309.5 4.6 %shard_map.302 = (f32[512,1024]{1,0:T(8,128)}, f32[128,4096]{1,0:T(8,128)}, f32[128,1024]{1,0:T(8,128)}, f32[128,1024]{1,0:T(8,128)}, f32[128,1024]{1,0:T(8,128)}, /*index=5*/f32[128,1024]{1,0:T(8,128)}) custom-call(s32[1]{0:T(128)} %bitcast.1.ctx, bf16[8,112,1024]{2,1,0:T(8,128)(2,1)S(1)} %all-to-all-done.8.mine, ...), custom_call_target="tpu_custom_call" | custom-call | flops 1000000 | bytes 10000000 | tf_op jit(solution)/shard_map/pallas_call | solution.py:262
  (229 shorter events, 55.4 us)
Async XLA Ops:
  0.7 14.1 %copy-start.1 = (bf16[128,4096]{1,0:T(8,128)(2,1)S(1)}, bf16[128,4096]{1,0:T(8,128)(2,1)}, u32[]{:S(2)}) copy-start(bf16[128,4096]{1,0:T(8,128)(2,1)} %w_up.1) | copy-start | bytes 3145732
  0.7 14.1 %copy-start.2 = (bf16[512,1024]{1,0:T(8,128)(2,1)S(1)}, bf16[512,1024]{1,0:T(8,128)(2,1)}, u32[]{:S(2)}) copy-start(bf16[512,1024]{1,0:T(8,128)(2,1)} %w_down.1) | copy-start | bytes 3145732
  6.1 12.6 %collective-permute-start = (bf16[128,1024]{1,0:T(8,128)(2,1)}, bf16[128,1024]{1,0:T(8,128)(2,1)S(1)}, u32[]{:S(2)}, u32[]{:S(2)}) collective-permute-start(bf16[128,1024]{1,0:T(8,128)(2,1)} %bitcast.190), channel_id=1, source_target_pairs={{0,16},{8,24},{16,0},{24,8},{32,48},{40,56},{48,32},{56,40},{64,80... | collective-permute-start | bytes 786440 | tf_op jit(solution)/shard_map/ppermute | solution.py:30
  9.7 14.1 %all-to-all-start = ((bf16[8,208,128]{2,1,0:T(8,128)(2,1)}), bf16[8,208,128]{2,1,0:T(8,128)(2,1)S(1)}, u32[]{:S(2)}, u32[]{:S(2)}) async-start(bf16[8,208,128]{2,1,0:T(8,128)(2,1)} %shard_map.296), calls=%async_computation | async-start | bytes 851968 | tf_op jit(solution)/shard_map/all_to_all | solution.py:46
  18.8 40.1 %copy-start = (bf16[256,1024]{1,0:T(8,128)(2,1)}, bf16[256,1024]{1,0:T(8,128)(2,1)S(1)}, u32[]{:S(2)}) copy-start(bf16[256,1024]{1,0:T(8,128)(2,1)S(1)} %pad_maximum_fusion.4.refs_0_) | copy-start | bytes 1572868
  23.8 50.6 %all-to-all-start.1 = ((bf16[8,240,1024]{2,1,0:T(8,128)(2,1)}), bf16[8,240,1024]{2,1,0:T(8,128)(2,1)}, u32[]{:S(2)}, u32[]{:S(2)}) async-start(bf16[8,240,1024]{2,1,0:T(8,128)(2,1)} %get-tuple-element.81), calls=%async_computation.1 | async-start | bytes 7864320 | tf_op jit(solution)/shard_map/all_to_all | solution.py:46
  28.3 13.2 %collective-permute-start.1 = (bf16[256,1024]{1,0:T(8,128)(2,1)S(1)}, bf16[256,1024]{1,0:T(8,128)(2,1)S(1)}, u32[]{:S(2)}, u32[]{:S(2)}) collective-permute-start(bf16[256,1024]{1,0:T(8,128)(2,1)S(1)} %pad_maximum_fusion.4.refs_0_), channel_id=1, source_target_pairs={{0,32},{8,40},{16,48},{24,56},{32,64},{40,72},{48,80},{56,88},{64,... | collective-permute-start | bytes 1572872 | tf_op jit(solution)/shard_map/ppermute | solution.py:34
  29.7 24.2 %collective-permute-start.2 = (bf16[256,1024]{1,0:T(8,128)(2,1)S(1)}, bf16[256,1024]{1,0:T(8,128)(2,1)S(1)}, u32[]{:S(2)}, u32[]{:S(2)}) collective-permute-start(bf16[256,1024]{1,0:T(8,128)(2,1)S(1)} %pad_maximum_fusion.4.refs_0_), channel_id=1, source_target_pairs={{0,64},{8,72},{16,80},{24,88},{32,96},{40,104},{48,112},{56,120},{... | collective-permute-start | bytes 1572872 | tf_op jit(solution)/shard_map/ppermute | solution.py:34
  32.3 24.1 %collective-permute-start.3 = (bf16[256,1024]{1,0:T(8,128)(2,1)S(1)}, bf16[256,1024]{1,0:T(8,128)(2,1)S(1)}, u32[]{:S(2)}, u32[]{:S(2)}) collective-permute-start(bf16[256,1024]{1,0:T(8,128)(2,1)S(1)} %pad_maximum_fusion.4.refs_0_), channel_id=1, source_target_pairs={{0,96},{8,104},{16,112},{24,120},{32,0},{40,8},{48,16},{56,24},{64... | collective-permute-start | bytes 1572872 | tf_op jit(solution)/shard_map/ppermute | solution.py:34
  33.5 24.0 %collective-permute-start.4 = (bf16[256,1024]{1,0:T(8,128)(2,1)S(1)}, bf16[256,1024]{1,0:T(8,128)(2,1)S(1)}, u32[]{:S(2)}, u32[]{:S(2)}) collective-permute-start(bf16[256,1024]{1,0:T(8,128)(2,1)S(1)} %pad_maximum_fusion.4.refs_0_), channel_id=1, source_target_pairs={{0,8},{8,0},{16,24},{24,16},{32,40},{40,32},{48,56},{56,48},{64,72... | collective-permute-start | bytes 1572872 | tf_op jit(solution)/shard_map/ppermute | solution.py:30
  41.6 31.2 %copy-start.5 = (bf16[256,1024]{1,0:T(8,128)(2,1)}, bf16[256,1024]{1,0:T(8,128)(2,1)S(1)}, u32[]{:S(2)}) copy-start(bf16[256,1024]{1,0:T(8,128)(2,1)S(1)} %collective-permute-done.1.refs_1_) | copy-start | bytes 1572868
  41.6 15.9 %collective-permute-start.5 = (bf16[256,1024]{1,0:T(8,128)(2,1)S(1)}, bf16[256,1024]{1,0:T(8,128)(2,1)}, u32[]{:S(2)}, u32[]{:S(2)}) collective-permute-start(bf16[256,1024]{1,0:T(8,128)(2,1)S(1)} %collective-permute-done.1.refs_1_), channel_id=1, source_target_pairs={{0,8},{8,0},{16,24},{24,16},{32,40},{40,32},{48,56},{56,48},{64,72... | collective-permute-start | bytes 1572872 | tf_op jit(solution)/shard_map/ppermute | solution.py:30
  53.9 18.9 %copy-start.6 = (bf16[256,1024]{1,0:T(8,128)(2,1)}, bf16[256,1024]{1,0:T(8,128)(2,1)S(1)}, u32[]{:S(2)}) copy-start(bf16[256,1024]{1,0:T(8,128)(2,1)S(1)} %collective-permute-done.2.refs_2_) | copy-start | bytes 1572868
  53.9 4.2 %collective-permute-start.6 = (bf16[256,1024]{1,0:T(8,128)(2,1)S(1)}, bf16[256,1024]{1,0:T(8,128)(2,1)}, u32[]{:S(2)}, u32[]{:S(2)}) collective-permute-start(bf16[256,1024]{1,0:T(8,128)(2,1)S(1)} %collective-permute-done.2.refs_2_), channel_id=1, source_target_pairs={{0,8},{8,0},{16,24},{24,16},{32,40},{40,32},{48,56},{56,48},{64,72... | collective-permute-start | bytes 1572872 | tf_op jit(solution)/shard_map/ppermute | solution.py:30
  56.4 2.4 collective-permute-start.7
  74.4 18.6 %copy-start.9 = (bf16[192,1024]{1,0:T(8,128)(2,1)}, bf16[192,1024]{1,0:T(8,128)(2,1)S(1)}, u32[]{:S(2)}) copy-start(bf16[192,1024]{1,0:T(8,128)(2,1)S(1)} %get-tuple-element.98.refs_8_) | copy-start | bytes 1179652
  76.8 21.4 %collective-permute-start.8 = (bf16[512,1024]{1,0:T(8,128)(2,1)}, bf16[512,1024]{1,0:T(8,128)(2,1)S(1)}, u32[]{:S(2)}, u32[]{:S(2)}) collective-permute-start(bf16[512,1024]{1,0:T(8,128)(2,1)} %bitcast.33), channel_id=1, source_target_pairs={{0,8},{8,0},{16,24},{24,16},{32,40},{40,32},{48,56},{56,48},{64,72... | collective-permute-start | bytes 3145736 | tf_op jit(solution)/shard_map/ppermute | solution.py:30
  78.2 14.7 %all-to-all-start.2 = ((bf16[16,64,128]{2,1,0:T(8,128)(2,1)}), bf16[16,64,128]{2,1,0:T(8,128)(2,1)S(1)}, u32[]{:S(2)}, u32[]{:S(2)}) async-start(bf16[16,64,128]{2,1,0:T(8,128)(2,1)} %get-tuple-element.83), calls=%async_computation.2 | async-start | bytes 524288 | tf_op jit(solution)/shard_map/all_to_all | solution.py:46
  92.9 21.1 %all-to-all-start.3 = ((bf16[8,80,1024]{2,1,0:T(8,128)(2,1)}), bf16[8,80,1024]{2,1,0:T(8,128)(2,1)S(1)}, u32[]{:S(2)}, u32[]{:S(2)}) async-start(bf16[8,80,1024]{2,1,0:T(8,128)(2,1)} %get-tuple-element.89), calls=%async_computation.3 | async-start | bytes 2621440 | tf_op jit(solution)/shard_map/all_to_all | solution.py:46
  99.0 6.9 %collective-permute-start.9 = (bf16[128,1024]{1,0:T(8,128)(2,1)S(1)}, bf16[128,1024]{1,0:T(8,128)(2,1)S(1)}, u32[]{:S(2)}, u32[]{:S(2)}) collective-permute-start(bf16[128,1024]{1,0:T(8,128)(2,1)S(1)} %fusion.27), channel_id=1, source_target_pairs={{0,32},{8,40},{16,48},{24,56},{32,0},{40,8},{48,16},{56,24},{64,96... | collective-permute-start | bytes 786440 | tf_op jit(solution)/shard_map/ppermute | solution.py:30
  106.8 8.8 %collective-permute-start.10 = (bf16[256,1024]{1,0:T(8,128)(2,1)}, bf16[256,1024]{1,0:T(8,128)(2,1)}, u32[]{:S(2)}, u32[]{:S(2)}) collective-permute-start(bf16[256,1024]{1,0:T(8,128)(2,1)} %pad_maximum_fusion.5), channel_id=1, source_target_pairs={{0,8},{8,0},{16,24},{24,16},{32,40},{40,32},{48,56},{56,48},{64,72... | collective-permute-start | bytes 1572872 | tf_op jit(solution)/shard_map/ppermute | solution.py:30
  110.5 6.1 %copy-start.43 = (f32[8,1,128]{2,1,0:T(1,128)S(1)}, f32[8,1,128]{2,1,0:T(1,128)}, u32[]{:S(2)}) copy-start(f32[8,1,128]{2,1,0:T(1,128)} %get-tuple-element.175) | copy-start | bytes 12292
  120.4 11.6 %copy-start.39 = (f32[8,1,128]{2,1,0:T(1,128)S(1)}, f32[8,1,128]{2,1,0:T(1,128)}, u32[]{:S(2)}) copy-start(f32[8,1,128]{2,1,0:T(1,128)} %get-tuple-element.176) | copy-start | bytes 12292
  120.4 11.6 %copy-start.41 = (f32[8,1,128]{2,1,0:T(1,128)S(1)}, f32[8,1,128]{2,1,0:T(1,128)}, u32[]{:S(2)}) copy-start(f32[8,1,128]{2,1,0:T(1,128)} %get-tuple-element.174) | copy-start | bytes 12292
  120.5 3.5 %collective-permute-start.11 = (bf16[256,1024]{1,0:T(8,128)(2,1)S(1)}, bf16[256,1024]{1,0:T(8,128)(2,1)S(1)}, u32[]{:S(2)}, u32[]{:S(2)}) collective-permute-start(bf16[256,1024]{1,0:T(8,128)(2,1)S(1)} %slice.310), channel_id=1, source_target_pairs={{0,8},{8,0},{16,24},{24,16},{32,40},{40,32},{48,56},{56,48},{64,72... | collective-permute-start | bytes 1572872 | tf_op jit(solution)/shard_map/ppermute | solution.py:30
  124.2 8.4 %copy-start.17 = (bf16[1,128,1024]{2,1,0:T(8,128)(2,1)S(1)}, bf16[1,128,1024]{2,1,0:T(8,128)(2,1)}, u32[]{:S(2)}) copy-start(bf16[1,128,1024]{2,1,0:T(8,128)(2,1)} %param.33) | copy-start | bytes 786436
  124.2 8.4 %copy-start.37 = (f32[8,1,128]{2,1,0:T(1,128)S(1)}, f32[8,1,128]{2,1,0:T(1,128)}, u32[]{:S(2)}) copy-start(f32[8,1,128]{2,1,0:T(1,128)} %get-tuple-element.172) | copy-start | bytes 12292
  124.3 7.8 %collective-permute-start.12 = (bf16[128,1024]{1,0:T(8,128)(2,1)S(1)}, bf16[128,1024]{1,0:T(8,128)(2,1)S(1)}, u32[]{:S(2)}, u32[]{:S(2)}) collective-permute-start(bf16[128,1024]{1,0:T(8,128)(2,1)S(1)} %slice.313), channel_id=1, source_target_pairs={{0,32},{8,40},{16,48},{24,56},{32,0},{40,8},{48,16},{56,24},{64,96... | collective-permute-start | bytes 786440 | tf_op jit(solution)/shard_map/ppermute | solution.py:30
  133.1 6.7 %collective-permute-start.13 = (bf16[128,1024]{1,0:T(8,128)(2,1)S(1)}, bf16[128,1024]{1,0:T(8,128)(2,1)S(1)}, u32[]{:S(2)}, u32[]{:S(2)}) collective-permute-start(bf16[128,1024]{1,0:T(8,128)(2,1)S(1)} %get-tuple-element.147), channel_id=1, source_target_pairs={{0,32},{8,40},{16,48},{24,56},{32,0},{40,8},{48,16},{56,24},{64,96... | collective-permute-start | bytes 786440 | tf_op jit(solution)/shard_map/ppermute | solution.py:30
  139.8 6.4 %copy-start.29 = (bf16[256,1024]{1,0:T(8,128)(2,1)}, bf16[256,1024]{1,0:T(8,128)(2,1)S(1)}, u32[]{:S(2)}) copy-start(bf16[256,1024]{1,0:T(8,128)(2,1)S(1)} %pad_maximum_fusion.6) | copy-start | bytes 1572868
  139.9 3.7 %collective-permute-start.14 = (bf16[256,1024]{1,0:T(8,128)(2,1)S(1)}, bf16[256,1024]{1,0:T(8,128)(2,1)S(1)}, u32[]{:S(2)}, u32[]{:S(2)}) collective-permute-start(bf16[256,1024]{1,0:T(8,128)(2,1)S(1)} %pad_maximum_fusion.6), channel_id=1, source_target_pairs={{0,8},{8,0},{16,24},{24,16},{32,40},{40,32},{48,56},{56,48},{64,72... | collective-permute-start | bytes 1572872 | tf_op jit(solution)/shard_map/ppermute | solution.py:30
  149.8 6.8 %collective-permute-start.15 = (bf16[256,1024]{1,0:T(8,128)(2,1)}, bf16[256,1024]{1,0:T(8,128)(2,1)S(1)}, u32[]{:S(2)}, u32[]{:S(2)}) collective-permute-start(bf16[256,1024]{1,0:T(8,128)(2,1)} %slice.309), channel_id=1, source_target_pairs={{0,8},{8,0},{16,24},{24,16},{32,40},{40,32},{48,56},{56,48},{64,72... | collective-permute-start | bytes 1572872 | tf_op jit(solution)/shard_map/ppermute | solution.py:30
  153.0 6.9 %copy-start.22 = (bf16[1024,1024]{1,0:T(8,128)(2,1)}, bf16[1024,1024]{1,0:T(8,128)(2,1)S(1)}, u32[]{:S(2)}) copy-start(bf16[1024,1024]{1,0:T(8,128)(2,1)S(1)} %convolution_convert_fusion) | copy-start | bytes 6291460
  153.0 3.6 %copy-start.26 = (f32[512,1024]{1,0:T(8,128)S(1)}, f32[512,1024]{1,0:T(8,128)}, u32[]{:S(2)}) copy-start(f32[512,1024]{1,0:T(8,128)} %copy-done.25) | copy-start | bytes 6291460
  154.0 3.3 %copy-start.47 = (bf16[512,1024]{1,0:T(8,128)(2,1)S(1)}, bf16[512,1024]{1,0:T(8,128)(2,1)}, u32[]{:S(2)}) copy-start(bf16[512,1024]{1,0:T(8,128)(2,1)} %copy-done.46) | copy-start | bytes 3145732
  154.0 14.6 %collective-permute-start.17 = (bf16[2,128,1024]{2,1,0:T(8,128)(2,1)S(1)}, bf16[2,128,1024]{2,1,0:T(8,128)(2,1)S(1)}, u32[]{:S(2)}, u32[]{:S(2)}) collective-permute-start(bf16[2,128,1024]{2,1,0:T(8,128)(2,1)S(1)} %get-tuple-element.156), channel_id=1, source_target_pairs={{0,2},{1,3},{2,4},{3,5},{4,6},{5,7},{6,0},{7,1},{8,10},{9,11},{10,... | collective-permute-start | bytes 1572872 | tf_op jit(solution)/shard_map/ppermute | solution.py:38
  154.0 14.6 %collective-permute-start.18 = (bf16[2,128,1024]{2,1,0:T(8,128)(2,1)S(1)}, bf16[2,128,1024]{2,1,0:T(8,128)(2,1)S(1)}, u32[]{:S(2)}, u32[]{:S(2)}) collective-permute-start(bf16[2,128,1024]{2,1,0:T(8,128)(2,1)S(1)} %get-tuple-element.155), channel_id=1, source_target_pairs={{0,6},{1,7},{2,0},{3,1},{4,2},{5,3},{6,4},{7,5},{8,14},{9,15},{10,... | collective-permute-start | bytes 1572872 | tf_op jit(solution)/shard_map/ppermute | solution.py:38
  156.8 7.2 %copy-start.40 = (f32[8,1,128]{2,1,0:T(1,128)S(1)}, f32[8,1,128]{2,1,0:T(1,128)}, u32[]{:S(2)}) copy-start(f32[8,1,128]{2,1,0:T(1,128)} %get-tuple-element.173) | copy-start | bytes 12292
  156.8 7.2 %collective-permute-start.16 = (bf16[128,1024]{1,0:T(8,128)(2,1)S(1)}, bf16[128,1024]{1,0:T(8,128)(2,1)S(1)}, u32[]{:S(2)}, u32[]{:S(2)}) collective-permute-start(bf16[128,1024]{1,0:T(8,128)(2,1)S(1)} %slice.312), channel_id=1, source_target_pairs={{0,32},{8,40},{16,48},{24,56},{32,0},{40,8},{48,16},{56,24},{64,96... | collective-permute-start | bytes 786440 | tf_op jit(solution)/shard_map/ppermute | solution.py:30
  166.4 5.1 %copy-start.15 = (bf16[128,1024]{1,0:T(8,128)(2,1)}, bf16[128,1024]{1,0:T(8,128)(2,1)S(1)}, u32[]{:S(2)}) copy-start(bf16[128,1024]{1,0:T(8,128)(2,1)S(1)} %get-tuple-element.91) | copy-start | bytes 786436
  172.2 7.0 %copy-start.16 = (bf16[128,1024]{1,0:T(8,128)(2,1)S(1)}, bf16[128,1024]{1,0:T(8,128)(2,1)}, u32[]{:S(2)}) copy-start(bf16[128,1024]{1,0:T(8,128)(2,1)} %copy-done.15) | copy-start | bytes 786436
  173.3 6.1 %collective-permute-start.19 = (bf16[8,64,1024]{2,1,0:T(8,128)(2,1)}, bf16[8,64,1024]{2,1,0:T(8,128)(2,1)}, u32[]{:S(2)}, u32[]{:S(2)}) collective-permute-start(bf16[8,64,1024]{2,1,0:T(8,128)(2,1)} %dynamic-slice_bitcast_fusion), channel_id=1, source_target_pairs={{0,8},{8,0},{16,24},{24,16},{32,40},{40,32},{48,56},{56,48},{64,72... | collective-permute-start | bytes 3145736 | tf_op jit(solution)/shard_map/ppermute | solution.py:30
  174.3 42.5 %collective-permute-start.30 = (bf16[2,128,1024]{2,1,0:T(8,128)(2,1)}, bf16[2,128,1024]{2,1,0:T(8,128)(2,1)}, u32[]{:S(2)}, u32[]{:S(2)}) collective-permute-start(bf16[2,128,1024]{2,1,0:T(8,128)(2,1)} %get-tuple-element.154), channel_id=1, source_target_pairs={{0,4},{1,5},{2,6},{3,7},{4,0},{5,1},{6,2},{7,3},{8,12},{9,13},{10,... | collective-permute-start | bytes 1572872 | tf_op jit(solution)/shard_map/ppermute | solution.py:38
  175.5 12.3 %all-to-all-start.4 = ((bf16[16,64,128]{2,1,0:T(8,128)(2,1)}), bf16[16,64,128]{2,1,0:T(8,128)(2,1)S(1)}, u32[]{:S(2)}, u32[]{:S(2)}) async-start(bf16[16,64,128]{2,1,0:T(8,128)(2,1)} %bitcast.54), calls=%async_computation.4 | async-start | bytes 524288 | tf_op jit(solution)/shard_map/all_to_all | solution.py:46
  184.2 32.6 %collective-permute-start.24 = (bf16[2,128,1024]{2,1,0:T(8,128)(2,1)}, bf16[2,128,1024]{2,1,0:T(8,128)(2,1)}, u32[]{:S(2)}, u32[]{:S(2)}) collective-permute-start(bf16[2,128,1024]{2,1,0:T(8,128)(2,1)} %get-tuple-element.159), channel_id=1, source_target_pairs={{0,2},{1,3},{2,4},{3,5},{4,6},{5,7},{6,0},{7,1},{8,10},{9,11},{10,... | collective-permute-start | bytes 1572872 | tf_op jit(solution)/shard_map/ppermute | solution.py:38
  186.2 31.0 %collective-permute-start.25 = (bf16[2,128,1024]{2,1,0:T(8,128)(2,1)}, bf16[2,128,1024]{2,1,0:T(8,128)(2,1)}, u32[]{:S(2)}, u32[]{:S(2)}) collective-permute-start(bf16[2,128,1024]{2,1,0:T(8,128)(2,1)} %get-tuple-element.158), channel_id=1, source_target_pairs={{0,6},{1,7},{2,0},{3,1},{4,2},{5,3},{6,4},{7,5},{8,14},{9,15},{10,... | collective-permute-start | bytes 1572872 | tf_op jit(solution)/shard_map/ppermute | solution.py:38
  187.9 32.9 %all-to-all-start.5 = ((bf16[4,144,1024]{2,1,0:T(8,128)(2,1)}), bf16[4,144,1024]{2,1,0:T(8,128)(2,1)S(1)}, u32[]{:S(2)}, u32[]{:S(2)}) async-start(bf16[4,144,1024]{2,1,0:T(8,128)(2,1)} %shard_map.299), calls=%async_computation.5 | async-start | bytes 2359296 | tf_op jit(solution)/shard_map/all_to_all | solution.py:46
  193.5 26.6 %collective-permute-start.26 = (bf16[2,128,1024]{2,1,0:T(8,128)(2,1)}, bf16[2,128,1024]{2,1,0:T(8,128)(2,1)}, u32[]{:S(2)}, u32[]{:S(2)}) collective-permute-start(bf16[2,128,1024]{2,1,0:T(8,128)(2,1)} %get-tuple-element.157), channel_id=1, source_target_pairs={{0,4},{1,5},{2,6},{3,7},{4,0},{5,1},{6,2},{7,3},{8,12},{9,13},{10,... | collective-permute-start | bytes 1572872 | tf_op jit(solution)/shard_map/ppermute | solution.py:38
  215.5 11.8 %collective-permute-start.20 = (bf16[256,1024]{1,0:T(8,128)(2,1)}, bf16[256,1024]{1,0:T(8,128)(2,1)}, u32[]{:S(2)}, u32[]{:S(2)}) collective-permute-start(bf16[256,1024]{1,0:T(8,128)(2,1)} %get-tuple-element.103), channel_id=1, source_target_pairs={{0,8},{8,0},{16,24},{24,16},{32,40},{40,32},{48,56},{56,48},{64,72... | collective-permute-start | bytes 1572872 | tf_op jit(solution)/shard_map/ppermute | solution.py:30
  216.7 10.6 %collective-permute-start.21 = (bf16[256,1024]{1,0:T(8,128)(2,1)}, bf16[256,1024]{1,0:T(8,128)(2,1)}, u32[]{:S(2)}, u32[]{:S(2)}) collective-permute-start(bf16[256,1024]{1,0:T(8,128)(2,1)} %get-tuple-element.104), channel_id=1, source_target_pairs={{0,8},{8,0},{16,24},{24,16},{32,40},{40,32},{48,56},{56,48},{64,72... | collective-permute-start | bytes 1572872 | tf_op jit(solution)/shard_map/ppermute | solution.py:30
  216.7 10.6 %collective-permute-start.22 = (bf16[256,1024]{1,0:T(8,128)(2,1)}, bf16[256,1024]{1,0:T(8,128)(2,1)}, u32[]{:S(2)}, u32[]{:S(2)}) collective-permute-start(bf16[256,1024]{1,0:T(8,128)(2,1)} %get-tuple-element.105), channel_id=1, source_target_pairs={{0,8},{8,0},{16,24},{24,16},{32,40},{40,32},{48,56},{56,48},{64,72... | collective-permute-start | bytes 1572872 | tf_op jit(solution)/shard_map/ppermute | solution.py:30
  217.3 10.1 %collective-permute-start.23 = (bf16[256,1024]{1,0:T(8,128)(2,1)}, bf16[256,1024]{1,0:T(8,128)(2,1)}, u32[]{:S(2)}, u32[]{:S(2)}) collective-permute-start(bf16[256,1024]{1,0:T(8,128)(2,1)} %get-tuple-element.106), channel_id=1, source_target_pairs={{0,8},{8,0},{16,24},{24,16},{32,40},{40,32},{48,56},{56,48},{64,72... | collective-permute-start | bytes 1572872 | tf_op jit(solution)/shard_map/ppermute | solution.py:30
  220.3 21.4 %collective-permute-start.31 = (bf16[128,1024]{1,0:T(8,128)(2,1)}, bf16[128,1024]{1,0:T(8,128)(2,1)}, u32[]{:S(2)}, u32[]{:S(2)}) collective-permute-start(bf16[128,1024]{1,0:T(8,128)(2,1)} %fusion.29), channel_id=1, source_target_pairs={{0,1},{1,0},{2,3},{3,2},{4,5},{5,4},{6,7},{7,6},{8,9},{9,8},{10,11... | collective-permute-start | bytes 786440 | tf_op jit(solution)/shard_map/ppermute | solution.py:42
  223.1 23.5 %all-to-all-start.6 = ((bf16[8,64,1024]{2,1,0:T(8,128)(2,1)}), bf16[8,64,1024]{2,1,0:T(8,128)(2,1)S(1)}, u32[]{:S(2)}, u32[]{:S(2)}) async-start(bf16[8,64,1024]{2,1,0:T(8,128)(2,1)} %shard_map.301), calls=%async_computation.6 | async-start | bytes 2097152 | tf_op jit(solution)/shard_map/all_to_all | solution.py:46
  229.4 24.4 %collective-permute-start.27 = (bf16[256,1024]{1,0:T(8,128)(2,1)}, bf16[256,1024]{1,0:T(8,128)(2,1)}, u32[]{:S(2)}, u32[]{:S(2)}) collective-permute-start(bf16[256,1024]{1,0:T(8,128)(2,1)} %add_convert_fusion.2), channel_id=1, source_target_pairs={{0,96},{8,104},{16,112},{24,120},{32,0},{40,8},{48,16},{56,24},{64... | collective-permute-start | bytes 1572872 | tf_op jit(solution)/shard_map/ppermute | solution.py:34
  234.4 7.2 %copy-start.20 = (f32[2,128,1024]{2,1,0:T(8,128)S(1)}, f32[2,128,1024]{2,1,0:T(8,128)}, u32[]{:S(2)}) copy-start(f32[2,128,1024]{2,1,0:T(8,128)} %copy-done.19) | copy-start | bytes 3145732
  234.4 19.4 %collective-permute-start.28 = (bf16[256,1024]{1,0:T(8,128)(2,1)}, bf16[256,1024]{1,0:T(8,128)(2,1)}, u32[]{:S(2)}, u32[]{:S(2)}) collective-permute-start(bf16[256,1024]{1,0:T(8,128)(2,1)} %add_convert_fusion.1), channel_id=1, source_target_pairs={{0,32},{8,40},{16,48},{24,56},{32,64},{40,72},{48,80},{56,88},{64,... | collective-permute-start | bytes 1572872 | tf_op jit(solution)/shard_map/ppermute | solution.py:34
  236.4 9.3 %collective-permute-start.32 = (bf16[128,1024]{1,0:T(8,128)(2,1)S(1)}, bf16[128,1024]{1,0:T(8,128)(2,1)S(1)}, u32[]{:S(2)}, u32[]{:S(2)}) collective-permute-start(bf16[128,1024]{1,0:T(8,128)(2,1)S(1)} %fusion.30), channel_id=1, source_target_pairs={{0,1},{1,0},{2,3},{3,2},{4,5},{5,4},{6,7},{7,6},{8,9},{9,8},{10,11... | collective-permute-start | bytes 786440 | tf_op jit(solution)/shard_map/ppermute | solution.py:42
  240.0 18.5 %collective-permute-start.29 = (bf16[256,1024]{1,0:T(8,128)(2,1)}, bf16[256,1024]{1,0:T(8,128)(2,1)}, u32[]{:S(2)}, u32[]{:S(2)}) collective-permute-start(bf16[256,1024]{1,0:T(8,128)(2,1)} %add_convert_fusion), channel_id=1, source_target_pairs={{0,64},{8,72},{16,80},{24,88},{32,96},{40,104},{48,112},{56,120},{... | collective-permute-start | bytes 1572872 | tf_op jit(solution)/shard_map/ppermute | solution.py:34
  246.8 15.8 %all-to-all-start.7 = ((bf16[4,64,1024]{2,1,0:T(8,128)(2,1)}), bf16[4,64,1024]{2,1,0:T(8,128)(2,1)S(1)}, u32[]{:S(2)}, u32[]{:S(2)}) async-start(bf16[4,64,1024]{2,1,0:T(8,128)(2,1)} %pad_maximum_fusion.7), calls=%async_computation.7 | async-start | bytes 1048576 | tf_op jit(solution)/shard_map/all_to_all | solution.py:46
  264.3 31.5 %copy-start.24 = (f32[128,1024]{1,0:T(8,128)S(1)}, f32[128,1024]{1,0:T(8,128)}, u32[]{:S(2)}) copy-start(f32[128,1024]{1,0:T(8,128)} %get-tuple-element.149) | copy-start | bytes 1572868
  264.3 32.3 %all-to-all-start.8 = ((bf16[8,112,1024]{2,1,0:T(8,128)(2,1)}), bf16[8,112,1024]{2,1,0:T(8,128)(2,1)S(1)}, u32[]{:S(2)}, u32[]{:S(2)}) async-start(bf16[8,112,1024]{2,1,0:T(8,128)(2,1)} %broadcast_in_dim.8), calls=%async_computation.8 | async-start | bytes 3670016 | tf_op jit(solution)/shard_map/all_to_all | solution.py:46
  271.0 24.7 %collective-permute-start.33 = (bf16[128,1024]{1,0:T(8,128)(2,1)S(1)}, bf16[128,1024]{1,0:T(8,128)(2,1)S(1)}, u32[]{:S(2)}, u32[]{:S(2)}) collective-permute-start(bf16[128,1024]{1,0:T(8,128)(2,1)S(1)} %slice.311), channel_id=1, source_target_pairs={{0,16},{8,24},{16,0},{24,8},{32,48},{40,56},{48,32},{56,40},{64,80... | collective-permute-start | bytes 786440 | tf_op jit(solution)/shard_map/ppermute | solution.py:30
  296.6 8.9 %collective-permute-start.34 = (bf16[8,112,1024]{2,1,0:T(8,128)(2,1)S(1)}, bf16[8,112,1024]{2,1,0:T(8,128)(2,1)}, u32[]{:S(2)}, u32[]{:S(2)}) collective-permute-start(bf16[8,112,1024]{2,1,0:T(8,128)(2,1)S(1)} %all-to-all-done.8.mine), channel_id=1, source_target_pairs={{0,8},{8,0},{16,24},{24,16},{32,40},{40,32},{48,56},{56,48},{64,72... | collective-permute-start | bytes 5505032 | tf_op jit(solution)/shard_map/ppermute | solution.py:30
  (28 other events, 46.2 us)
